TPU v7x, 512 devices: a whole 4x8x8 slice. The times are simulated.
512 devices in a mesh: af: 128 (over x, y, z_lo), row: 4 (over z_hi, core).
Axes of the slice: x: 4, y: 8, z: 8 (z_hi: 2, z_lo: 4; z = z_hi * 4 + z_lo), core: 2. Of those that a mesh axis runs over, the one named last changes fastest.
Arguments:
- traces: bfloat16 [1024, 1024, 512], P('af', 'row'), may hold values from -6 to 6
- live: int32 [1024, 1024], P('af', 'row'), may hold values 0 or 1
- selected: int32 [32], replicated, may hold values from 0 to 1023, as said below
Outputs:
- multiples: float32 [32, 4, 256, 512], P(None, 'row', 'af')
Inputs may be any that keep to these rules, and one draw needn't show every extreme that they name: `selected`: 32 different shot numbers in no particular order; 0 and 1023 are always among them.
All inputs are finite; a program needn't handle non-finite values. No bound on the sum of `live` on one device may be relied on, other than what follows from the above.
Results may differ from a plain program's by a relative error of at most 0.0074.
Values may be sent and summed in bfloat16 or wider, within the bound.
A program may use at most 64 MiB of HBM per device.

v0:
```python
import math

import jax
import jax.numpy as jnp
from jax import lax
from jax.sharding import PartitionSpec as P

NF = 256


def tables(samples, freqs):
    times_idx = jnp.arange(samples, dtype=jnp.int32)
    freq_idx = jnp.arange(freqs, dtype=jnp.int32)
    phases = (times_idx[:, None] * freq_idx[None, :] % samples).astype(jnp.float32) * (
        2.0 * math.pi / samples
    )
    norm_factor = 1.0 / math.sqrt(samples)
    forward = (jnp.concatenate([jnp.cos(phases), -jnp.sin(phases)], axis=1) * norm_factor).astype(
        jnp.bfloat16
    )
    weights = jnp.where(freq_idx == 0, 1.0, 2.0).astype(jnp.float32)
    inverse = jnp.concatenate(
        [jnp.cos(phases) * weights[None, :], -jnp.sin(phases) * weights[None, :]], axis=1
    )
    inverse = (inverse.T * norm_factor).astype(jnp.bfloat16)
    return (forward, inverse)


def per_device(traces, live, selected):
    shot_count, recv_block, samples = traces.shape
    groups = lax.axis_size("af")
    stations = shot_count * groups
    per_group = NF // groups
    factor = 1.0 / math.sqrt(stations)
    forward, inverse = tables(samples, NF)
    masked = traces * live[:, :, None].astype(jnp.bfloat16)
    spectra = jnp.einsum("nc,srn->scr", forward, masked, preferred_element_type=jnp.float32).astype(
        jnp.bfloat16
    )
    spectra = spectra.reshape(shot_count, 2, groups, per_group, recv_block)
    regrouped = lax.all_to_all(spectra, "af", split_axis=2, concat_axis=0, tiled=True)
    chosen = jnp.take(regrouped, selected, axis=0)
    chosen = lax.all_gather(chosen, "row", axis=4, tiled=True)
    sel_real = chosen[:, 0, 0]
    sel_imag = chosen[:, 1, 0]
    all_real = regrouped[:, 0, 0]
    all_imag = regrouped[:, 1, 0]
    part_real = (
        jnp.einsum("onk,knr->onr", sel_real, all_real, preferred_element_type=jnp.float32)
        - jnp.einsum("onk,knr->onr", sel_imag, all_imag, preferred_element_type=jnp.float32)
    ) * factor
    part_imag = (
        jnp.einsum("onk,knr->onr", sel_real, all_imag, preferred_element_type=jnp.float32)
        + jnp.einsum("onk,knr->onr", sel_imag, all_real, preferred_element_type=jnp.float32)
    ) * factor
    predicted = jnp.stack([part_real.astype(jnp.bfloat16), part_imag.astype(jnp.bfloat16)], axis=1)
    returned = lax.all_to_all(predicted, "af", split_axis=3, concat_axis=2, tiled=True)
    shots_here = returned.shape[0]
    recv_here = returned.shape[3]
    flat = returned.reshape(shots_here, 2 * NF, recv_here)
    result = jnp.einsum("ocr,ct->ort", flat, inverse, preferred_element_type=jnp.float32)
    return result[:, None]


def solution(mesh):
    in_specs = (P("af", "row", None), P("af", "row"), P())
    out_specs = P(None, "row", "af", None)
    return jax.shard_map(
        per_device, mesh=mesh, in_specs=in_specs, out_specs=out_specs, check_vma=False
    )
```

profile of v0, /device:TPU:1, one launch (start us, length us, event | category | flops | bytes accessed | tf_op | source)
XLA Modules:
  0.0 126.0 jit_solution(10062450488086756237)
XLA Ops:
  0.0 2.1 %sine_negate_fusion = (f32[512,256]{1,0:T(8,128)S(1)}, f32[512,256]{1,0:T(8,128)S(1)}) fusion(), kind=kLoop, calls=%fused_computation.34 | loop fusion | flops 1966080 | bytes 1048576 | tf_op jit(solution)/shard_map/neg | solution.py:18
  2.1 0.7 convert_element_type.38
  2.8 4.2 %convert_bitcast_fusion = bf16[8,512,256]{1,2,0:T(8,128)(2,1)} fusion(bf16[8,256,512]{2,1,0:T(8,128)(2,1)} %param.3, bf16[8,256]{1,0:T(8,128)(2,1)S(1)} %convert_element_type.38, f32[512,256]{1,0:T(8,128)S(1)} %get-tuple-element.9, f32[512,256]{1,0:T(8,128)S(1)} %get-tuple-element.10), kind=kOutput, calls=%fused_computation.1 | convolution fusion | flops 1076625408 | bytes 5246976 | tf_op jit(solution)/shard_map/nc,srn->scr/dot_general | solution.py:37
  7.0 3.3 %copy.16 = bf16[8,512,256]{2,0,1:T(8,128)(2,1)S(1)} copy(bf16[8,512,256]{1,2,0:T(8,128)(2,1)} %convert_bitcast_fusion) | data formatting | bytes 4194304 | tf_op jit(solution)/shard_map/convert_element_type | solution.py:37
  10.4 1.7 %copy.17 = bf16[8,2,128,2,256]{4,0,3,1,2:T(8,128)(2,1)} copy(bf16[8,2,128,2,256]{4,0,3,2,1:T(8,128)(2,1)S(1)} %bitcast.59) | data formatting | bytes 4194304 | tf_op jit(solution)/shard_map/reshape | solution.py:40
  12.0 0.0 copy-start.2
  12.0 17.9 %all-to-all-start = ((bf16[8,2,128,2,256]{4,0,3,1,2:T(8,128)(2,1)}), bf16[8,2,128,2,256]{4,0,3,1,2:T(8,128)(2,1)S(1)}, u32[]{:S(2)}, u32[]{:S(2)}) async-start(bf16[8,2,128,2,256]{4,0,3,1,2:T(8,128)(2,1)} %copy.17), calls=%async_computation | async-start | bytes 4194304 | tf_op jit(solution)/shard_map/all_to_all | solution.py:41
  30.0 0.0 copy-done.2
  30.0 48.8 %all-to-all-done = bf16[8,2,128,2,256]{4,0,3,1,2:T(8,128)(2,1)S(1)} async-done(((bf16[8,2,128,2,256]{4,0,3,1,2:T(8,128)(2,1)}), bf16[8,2,128,2,256]{4,0,3,1,2:T(8,128)(2,1)S(1)}, u32[]{:S(2)}, u32[]{:S(2)}) %all-to-all-start) | async-done | bytes 2097184 | tf_op jit(solution)/shard_map/all_to_all | solution.py:41
  78.8 0.1 copy.30
  78.9 0.0 copy-start
  78.9 1.3 %copy-done = bf16[8,2,128,2,256]{4,0,2,3,1:T(8,128)(2,1)} copy-done((bf16[8,2,128,2,256]{4,0,2,3,1:T(8,128)(2,1)}, bf16[8,2,128,2,256]{4,0,2,3,1:T(8,128)(2,1)S(1)}, u32[]{:S(2)}) %copy-start) | copy-done | bytes 2097176
  80.3 3.5 %copy.19 = bf16[1024,2,2,256]{3,2,1,0:T(2,128)(2,1)} copy(bf16[1024,2,2,256]{3,0,2,1:T(8,128)(2,1)S(1)} %bitcast.54) | data formatting | bytes 4194304 | tf_op jit(solution)/shard_map/all_to_all | solution.py:41
  83.7 0.0 copy-start.1
  83.7 2.4 %gather_fusion = bf16[32,2,2,256]{3,2,1,0:T(2,128)(2,1)S(1)} fusion(bf16[1024,2,2,256]{3,2,1,0:T(2,128)(2,1)} %copy.19, s32[1024]{0:T(1024)S(1)} %pad_clamp_fusion), kind=kCustom, calls=%fused_computation | custom fusion | bytes 131200 | tf_op jit(solution)/shard_map/jit(_take)/gather | solution.py:42
  86.2 0.1 bitcast_select_fusion
  86.2 15.0 %all_gather.3 = bf16[32,2,1,2,1024]{4,0,3,2,1:T(8,128)(2,1)S(1)} all-gather(bf16[32,2,1,2,256]{4,0,3,2,1:T(8,128)(2,1)S(1)} %bitcast_select_fusion), channel_id=1, replica_groups=mesh['af'=128,'row'=4] {'row'}, dimensions={4}, use_global_device_ids=true | all-gather | bytes 327680 | tf_op jit(solution)/shard_map/all_gather | solution.py:43
  101.2 1.5 %fusion.13 = f32[2,256,32]{1,2,0:T(8,128)S(1)} fusion(bf16[1024,2,1,2,256]{4,0,3,2,1:T(8,128)(2,1)} %bitcast.55, bf16[32,2,1,2,1024]{4,0,3,2,1:T(8,128)(2,1)S(1)} %all_gather.3), kind=kOutput, calls=%fused_computation.22 | convolution fusion | flops 33554432 | bytes 1245184 | tf_op jit(solution)/shard_map/onk,knr->onr/dot_general | solution.py:49
  102.7 1.5 %fusion.14 = f32[2,256,32]{1,2,0:T(8,128)S(1)} fusion(bf16[1024,2,1,2,256]{4,0,3,2,1:T(8,128)(2,1)} %bitcast.56, bf16[32,2,1,2,1024]{4,0,3,2,1:T(8,128)(2,1)S(1)} %all_gather.3), kind=kOutput, calls=%fused_computation.23 | convolution fusion | flops 33554432 | bytes 1245184 | tf_op jit(solution)/shard_map/onk,knr->onr/dot_general | solution.py:53
  104.2 0.0 copy-done.1
  104.2 0.3 fusion.9
  104.5 0.3 fusion.8
  104.8 0.2 copy.21
  105.0 0.8 reshape.43
  105.8 8.1 %all-to-all-start.1 = ((bf16[128,2,128]{2,1,0:T(2,128)(2,1)}), bf16[128,2,128]{2,1,0:T(2,128)(2,1)S(1)}, u32[]{:S(2)}, u32[]{:S(2)}) async-start(bf16[128,2,128]{2,1,0:T(2,128)(2,1)} %reshape.43), calls=%async_computation.1 | async-start | bytes 131072 | tf_op jit(solution)/shard_map/all_to_all | solution.py:57
  113.9 2.1 %broadcast_multiply_fusion.1 = (f32[512,256]{1,0:T(8,128)S(1)}, f32[512,256]{1,0:T(8,128)S(1)}) fusion(f32[256]{0:T(256)S(1)} %compare_select_fusion.1), kind=kLoop, calls=%fused_computation.39 | loop fusion | flops 2228224 | bytes 1049600 | tf_op jit(solution)/shard_map/mul | solution.py:23
  116.0 8.4 %all-to-all-done.1 = bf16[128,2,128]{2,1,0:T(2,128)(2,1)S(1)} async-done(((bf16[128,2,128]{2,1,0:T(2,128)(2,1)}), bf16[128,2,128]{2,1,0:T(2,128)(2,1)S(1)}, u32[]{:S(2)}, u32[]{:S(2)}) %all-to-all-start.1) | async-done | bytes 65568 | tf_op jit(solution)/shard_map/all_to_all | solution.py:57
  124.4 0.2 reshape.44
  124.6 0.3 copy.23
  124.9 0.3 convolution_bitcast_fusion
  125.2 0.8 copy.25
  (6 shorter events, 0.1 us)
Async XLA Ops:
  12.0 17.9 %copy-start.2 = (s32[32]{0:T(128)S(1)}, s32[32]{0:T(128)}, u32[]{:S(2)}) copy-start(s32[32]{0:T(128)} %param.5) | copy-start | bytes 388
  12.0 66.7 %all-to-all-start = ((bf16[8,2,128,2,256]{4,0,3,1,2:T(8,128)(2,1)}), bf16[8,2,128,2,256]{4,0,3,1,2:T(8,128)(2,1)S(1)}, u32[]{:S(2)}, u32[]{:S(2)}) async-start(bf16[8,2,128,2,256]{4,0,3,1,2:T(8,128)(2,1)} %copy.17), calls=%async_computation | async-start | bytes 4194304 | tf_op jit(solution)/shard_map/all_to_all | solution.py:41
  78.9 1.3 %copy-start = (bf16[8,2,128,2,256]{4,0,2,3,1:T(8,128)(2,1)}, bf16[8,2,128,2,256]{4,0,2,3,1:T(8,128)(2,1)S(1)}, u32[]{:S(2)}) copy-start(bf16[8,2,128,2,256]{4,0,2,3,1:T(8,128)(2,1)S(1)} %copy.30) | copy-start | bytes 6291460
  83.7 20.5 %copy-start.1 = (bf16[8,2,128,2,256]{4,0,2,3,1:T(8,128)(2,1)S(1)}, bf16[8,2,128,2,256]{4,0,2,3,1:T(8,128)(2,1)}, u32[]{:S(2)}) copy-start(bf16[8,2,128,2,256]{4,0,2,3,1:T(8,128)(2,1)} %copy-done) | copy-start | bytes 6291460
  105.8 18.6 %all-to-all-start.1 = ((bf16[128,2,128]{2,1,0:T(2,128)(2,1)}), bf16[128,2,128]{2,1,0:T(2,128)(2,1)S(1)}, u32[]{:S(2)}, u32[]{:S(2)}) async-start(bf16[128,2,128]{2,1,0:T(2,128)(2,1)} %reshape.43), calls=%async_computation.1 | async-start | bytes 131072 | tf_op jit(solution)/shard_map/all_to_all | solution.py:57
where the time goes:
time: 126 us
  waiting for transfers between devices  57.2 us (45%)
  starting transfers between devices  26 us (21%)
  blocking collectives  15 us (12%)
  local copies, waits for them, and re-layouts  14.6 us (12%)
  matrix products  8.15 us (6%)
  other arithmetic  4.99 us (4%)
    all_to_all x1, waiting for transfers between devices, per_device(): lax.all_to_all(spectra, 'af', split_axis=2, concat_axis=0, tiled=True)  48.8 us
    all_to_all x1, starting transfers between devices, per_device(): lax.all_to_all(spectra, 'af', split_axis=2, concat_axis=0, tiled=True)  17.9 us
    all_gather x1, blocking collectives, per_device(): chosen = lax.all_gather(chosen, 'row', axis=4, tiled=True)  15 us
    all_to_all x1, waiting for transfers between devices, per_device(): lax.all_to_all(predicted, 'af', split_axis=3, concat_axis=2, tiled=True)  8.43 us
    all_to_all x1, starting transfers between devices, per_device(): lax.all_to_all(predicted, 'af', split_axis=3, concat_axis=2, tiled=True)  8.06 us
    dot_general x1, matrix products, per_device(): jnp.einsum('nc,srn->scr', forward, masked, preferred_element_type=jnp.flo...  4.25 us
    all_to_all x2, local copies, waits for them, and re-layouts, per_device(): lax.all_to_all(spectra, 'af', split_axis=2, concat_axis=0, tiled=True)  3.6 us
    convert_element_type x1, local copies, waits for them, and re-layouts, per_device(): jnp.einsum('nc,srn->scr', forward, masked, preferred_element_type=jnp.flo...  3.33 us
  transfers between devices with their start and end apart: 2, of which 2 were waited for; matrix products, arithmetic and copies ran while one was open for 2% of the time, Pallas kernels for 0%

commit v1 on v0

v1 whole, which is shorter than its diff:
```python
import functools
import math

import jax
import jax.numpy as jnp
import numpy as np
from jax import lax
from jax.experimental import pallas as pl
from jax.experimental.pallas import tpu as pltpu
from jax.sharding import PartitionSpec as P

MESH = pl.DeviceIdType.MESH
BF, F32, I32 = jnp.bfloat16, jnp.float32, jnp.int32

NX, NY, NZ, NROW = 4, 8, 4, 4
NT, NF, SHOTS, RECV, OUT = 512, 256, 8, 256, 32
BANDS, PER = 32, 8
COMP = 2 * PER


def host_tables():
    t = np.arange(NT)[:, None]
    f = np.arange(NF)[None, :]
    ang = (t * f % NT) * (2.0 * math.pi / NT)
    norm = 1.0 / math.sqrt(NT)
    w = np.where(np.arange(NF) == 0, 1.0, 2.0)[:, None]
    cos, sin = np.cos(ang).T, -np.sin(ang).T
    fwd = np.stack([cos.reshape(BANDS, PER, NT), sin.reshape(BANDS, PER, NT)], axis=1) * norm
    inv = np.concatenate([cos * w, sin * w], axis=0) * norm
    as_bf = lambda a: a.astype(np.float32).astype(jnp.bfloat16)
    return as_bf(fwd.reshape(2 * NF, NT)), as_bf(inv)


def af(x, y, z):
    return (x * NY + y) * NZ + z


def base_of(y):
    return (y - 2 + y % 2 + NY) % NY


def iota(shape, dim):
    return lax.broadcasted_iota(I32, shape, dim)


def mm(a, b, dims=((1,), (0,))):
    return lax.dot_general(a, b, (dims, ((), ())), preferred_element_type=F32)


def kernel(
    sel_ref, traces_hbm, live_ref, fwd_hbm, inv_hbm, out_ref,
    traces, fwd, inv, send, recv, bt, perm, pick, lanes, spread,
    a_own, a_msg, a_in, a_row, p2, stage, r_send, r_recv,
    load_sem, send_sem, recv_sem, own_sem, a_send_sem, a_recv_sem, row_send_sem, row_recv_sem,
    r_send_sem, r_recv_sem, r_own_sem,
):
    a = lax.axis_index("af")
    row = lax.axis_index("row")
    x, y, z = a // (NY * NZ), (a // NZ) % NY, a % NZ
    half = y // 2
    zp, zs = z // 2, z % 2
    base = base_of(y)
    cores = (a, row // 2 * 2 + 1 - row % 2)
    across = (a, (row + 2) % NROW)

    def home(u):
        return af(x, (y + 4 * (u // 2)) % NY, (z + 2 * (u % 2)) % NZ)

    fwd_copy = pltpu.make_async_copy(fwd_hbm, fwd, load_sem.at[SHOTS])
    inv_copy = pltpu.make_async_copy(inv_hbm, inv, load_sem.at[SHOTS + 1])
    fwd_copy.start()
    loads = [pltpu.make_async_copy(traces_hbm.at[s], traces.at[s], load_sem.at[s]) for s in range(SHOTS)]
    for c in loads:
        c.start()
    inv_copy.start()

    barrier = pltpu.get_barrier_semaphore()

    @pl.loop(1, BANDS)
    def _(i):
        sx = (x + i // 8) % NX
        sy = (base + ((y - base + NY) % NY + (i // 2) % 4) % 4) % NY
        sz = 2 * zp + (zs + i) % 2
        pl.semaphore_signal(barrier, inc=1, device_id=(af(sx, sy, sz), row), device_id_type=MESH)

    @pl.loop(1, 4)
    def _(u):
        pl.semaphore_signal(barrier, inc=1, device_id=(home(u), row), device_id_type=MESH)

    pl.semaphore_signal(barrier, inc=1, device_id=cores, device_id_type=MESH)
    pl.semaphore_signal(barrier, inc=1, device_id=across, device_id_type=MESH)

    fwd_copy.wait()
    for c in loads:
        c.wait()
    live = live_ref[...].astype(F32)

    def band_copy(dx, w, dz):
        bx = (x + dx) % NX
        hy = (2 * half - 1 + (y % 2 + 1 + w) % 4 + NY) % NY
        bz = (zs + dz) % 2
        band = bx * 8 + (hy % 4) * 2 + bz
        slot = x * 8 + ((y - base_of(hy) + NY) % NY) * 2 + zs
        return pltpu.make_async_remote_copy(
            src_ref=send.at[band], dst_ref=recv.at[slot], send_sem=send_sem,
            recv_sem=recv_sem.at[slot], device_id=(af(bx, hy, 2 * zp + bz), row), device_id_type=MESH,
        )

    own_band = x * 8 + (y % 4) * 2 + zs
    own_slot = x * 8 + ((y - base + NY) % NY) * 2 + zs
    own_copy = pltpu.make_async_copy(send.at[own_band], recv.at[own_slot], own_sem)

    @pl.loop(0, NX)
    def _(i):
        dx = (i + 1) % NX
        bx = (x + dx) % NX
        table = fwd[pl.ds(pl.multiple_of(bx * 128, 128), 128), :]
        for s in range(SHOTS):
            spec = mm(table, traces[s], ((1,), (1,))) * live[s : s + 1, :]
            send[pl.ds(bx * 8, 8), s] = spec.astype(BF).reshape(8, COMP, RECV)

        @pl.when(i == 0)
        def _():
            pl.semaphore_wait(barrier, BANDS - 1 + 3 + 2)

        @pl.loop(0, 8)
        def _(j):
            w, dz = j // 2, j % 2

            @pl.when(dx + j != 0)
            def _():
                band_copy(dx, w, dz).start()

    own_copy.start()

    ro, co = iota((256, 256), 0), iota((256, 256), 1)
    perm[...] = jnp.where(co == (ro % 16) // 8 * 128 + ro % 8 * 16 + ro // 16, 1.0, 0.0).astype(BF)
    j = iota((1, 512), 1)
    k64 = j % 64
    shot = ((j // 128 * NY + (base + k64 // 16) % NY) * NZ + 2 * zp + k64 // 8 % 2) * SHOTS + k64 % 8
    part = j % 128 // 64
    o_at = iota((OUT, 512), 0)
    want = jnp.full((OUT, 512), -1, I32)
    for o in range(OUT):
        want = jnp.where(o_at == o, sel_ref[o], want)
    hit = want == shot
    pick[0:OUT, :] = jnp.where(hit & (part == 0), 1.0, 0.0).astype(BF)
    pick[OUT : 2 * OUT, :] = jnp.where(hit & (part == 1), 1.0, 0.0).astype(BF)
    u = j // 128
    k_here = ((base + 4 * (u // 2) + k64 // 16) % NY * NZ + 2 * ((zp + u) % 2) + k64 // 8 % 2) * 8 + k64 % 8
    from_row = part * RECV + k_here
    lanes[...] = jnp.where(iota((512, 512), 0) == from_row, 1.0, 0.0).astype(BF)
    d_at = iota((128, 512), 0)
    j2 = iota((128, 512), 1)
    spread[...] = jnp.where(j2 % 256 == 2 * d_at + j2 // 256, 1.0, 0.0).astype(BF)
    p2[...] = jnp.zeros_like(p2)

    own_copy.wait()

    @pl.loop(0, NX)
    def _(i):
        sx = (x + 2 * NX - 1 - i) % NX

        @pl.loop(0, 4)
        def _(ys):
            for b in range(2):
                slot = sx * 8 + ys * 2 + b

                @pl.when(slot != own_slot)
                def _():
                    pltpu.make_async_remote_copy(
                        src_ref=send.at[0], dst_ref=recv.at[slot], send_sem=send_sem,
                        recv_sem=recv_sem.at[slot], device_id=cores, device_id_type=MESH,
                    ).wait_recv()

            block = recv[pl.ds(sx * 8 + ys * 2, 2)].reshape(256, RECV)
            turned = mm(perm[...], block).astype(BF).reshape(2, PER, 16, RECV)
            bt[:, sx, 0, ys] = turned[0]
            bt[:, sx, 1, ys] = turned[1]

    for f in range(PER):
        got = mm(pick[...], bt[f].reshape(512, RECV)).astype(BF)
        a_own[f * OUT : (f + 1) * OUT, 0:RECV] = got[0:OUT]
        a_own[f * OUT : (f + 1) * OUT, RECV:] = got[OUT:]
    for v in range(4):
        a_msg[v] = mm(a_own[...], lanes[:, v * 128 : (v + 1) * 128]).astype(BF)

    def home_copy(v):
        return pltpu.make_async_remote_copy(
            src_ref=a_msg.at[v], dst_ref=a_in.at[v], send_sem=a_send_sem.at[v],
            recv_sem=a_recv_sem.at[v], device_id=(home(v), row), device_id_type=MESH,
        )

    for v in (3, 2, 1):
        home_copy(v).start()
    for v in (1, 2, 3):
        home_copy(v).wait()
    a_row[row] = a_msg[0] + a_in[1] + a_in[2] + a_in[3]

    other = (row + 2) % NROW

    def row_copy(slot, to, sem):
        return pltpu.make_async_remote_copy(
            src_ref=a_row.at[slot], dst_ref=a_row.at[slot], send_sem=row_send_sem.at[sem],
            recv_sem=row_recv_sem.at[sem], device_id=to, device_id_type=MESH,
        )

    first, second, third = row_copy(row, across, 0), row_copy(row, cores, 1), row_copy(other, cores, 2)
    first.start()
    second.start()
    first.wait_recv()
    third.start()
    second.wait_recv()
    third.wait_recv()

    sign = jnp.where(iota((1, 128), 1) < 64, 1.0, -1.0)
    left = []
    for v in range(NROW):
        val = a_row[v].astype(F32)
        left.append(((val * sign).astype(BF), pltpu.roll(val, 64, 1).astype(BF)))
    factor = 1.0 / math.sqrt(NX * NY * NZ * SHOTS)
    for f in range(PER):
        rows = slice(f * OUT, (f + 1) * OUT)
        lhs = jnp.concatenate(
            [jnp.concatenate([left[v][part_][rows] for v in range(NROW)], axis=1) for part_ in range(2)], axis=0
        )
        pred = (mm(lhs, bt[f].reshape(512, RECV)) * factor).astype(BF)
        p2[f, 0:64, 0:RECV] = pred
        p2[f, 64:128, RECV:] = pred

    for f in range(PER):
        stage[pl.ds(f, 128, stride=8), :] = mm(spread[...], p2[f], ((1,), (1,)))
    r_send[...] = stage[...].astype(BF).reshape(128, 8, 128)

    my_slot = (y // 4 * 2 + zp) * BANDS + own_band
    own_r = pltpu.make_async_copy(r_send.at[a], r_recv.at[my_slot], r_own_sem)
    own_r.start()

    @pl.loop(1, 128)
    def _(i):
        d = (a + i * 47) % 128
        pltpu.make_async_remote_copy(
            src_ref=r_send.at[d], dst_ref=r_recv.at[my_slot], send_sem=r_send_sem,
            recv_sem=r_recv_sem, device_id=(d, row), device_id_type=MESH,
        ).start()

    all_r = pltpu.make_async_remote_copy(
        src_ref=r_send.at[pl.ds(0, 127)], dst_ref=r_recv.at[pl.ds(0, 127)], send_sem=r_send_sem,
        recv_sem=r_recv_sem, device_id=cores, device_id_type=MESH,
    )
    inv_copy.wait()
    own_r.wait()
    all_r.wait_recv()

    total = r_recv[0:32].astype(F32)
    for v in range(1, 4):
        total = total + r_recv[v * 32 : (v + 1) * 32].astype(F32)
    turned = total.reshape(256, 128).T.astype(BF)
    lhs = jnp.concatenate(
        [jnp.concatenate([turned[r * 64 : r * 64 + 32], turned[r * 64 + 32 : r * 64 + 64]], axis=1) for r in range(2)],
        axis=0,
    )
    res = mm(lhs, inv[...])
    for r in range(2):
        out_ref[r] = res[r * 32 : (r + 1) * 32]

    all_r.wait_send()
    for c in (first, second, third):
        c.wait_send()
    pltpu.make_async_remote_copy(
        src_ref=send.at[pl.ds(0, 31)], dst_ref=recv.at[pl.ds(0, 31)], send_sem=send_sem,
        recv_sem=recv_sem.at[0], device_id=cores, device_id_type=MESH,
    ).wait_send()


def per_device(traces, live, selected):
    fwd, inv = host_tables()
    any_, vmem = pl.BlockSpec(memory_space=pl.ANY), pl.BlockSpec(memory_space=pltpu.VMEM)
    dma = pltpu.SemaphoreType.DMA
    out = pl.pallas_call(
        kernel,
        out_shape=jax.ShapeDtypeStruct((2, OUT, NT), F32),
        in_specs=[pl.BlockSpec(memory_space=pltpu.SMEM), any_, vmem, any_, any_],
        out_specs=vmem,
        scratch_shapes=[
            pltpu.VMEM((SHOTS, RECV, NT), BF),
            pltpu.VMEM((2 * NF, NT), BF),
            pltpu.VMEM((2 * NF, NT), BF),
            pltpu.VMEM((BANDS, SHOTS, COMP, RECV), BF),
            pltpu.VMEM((BANDS, SHOTS, COMP, RECV), BF),
            pltpu.VMEM((PER, NX, 2, 4, 16, RECV), BF),
            pltpu.VMEM((256, 256), BF),
            pltpu.VMEM((2 * OUT, 512), BF),
            pltpu.VMEM((512, 512), BF),
            pltpu.VMEM((128, 512), BF),
            pltpu.VMEM((PER * OUT, 512), BF),
            pltpu.VMEM((4, PER * OUT, 128), BF),
            pltpu.VMEM((4, PER * OUT, 128), BF),
            pltpu.VMEM((NROW, PER * OUT, 128), BF),
            pltpu.VMEM((PER, 128, 512), BF),
            pltpu.VMEM((1024, 128), F32),
            pltpu.VMEM((128, 8, 128), BF),
            pltpu.VMEM((128, 8, 128), BF),
            dma((SHOTS + 2,)), dma, dma((BANDS,)), dma, dma((4,)), dma((4,)), dma((3,)), dma((3,)),
            dma, dma, dma,
        ],
        compiler_params=pltpu.CompilerParams(
            collective_id=0, has_side_effects=True, vmem_limit_bytes=40 << 20
        ),
        cost_estimate=pl.CostEstimate(flops=2 << 30, bytes_accessed=4 << 20, transcendentals=0),
        name="multiples",
    )(selected, traces, live, jnp.asarray(fwd), jnp.asarray(inv))
    return out.transpose(1, 0, 2)[:, None]


def solution(mesh):
    in_specs = (P("af", "row", None), P("af", "row"), P())
    out_specs = P(None, "row", "af", None)
    return jax.shard_map(per_device, mesh=mesh, in_specs=in_specs, out_specs=out_specs, check_vma=False)
```

time: 126 us -> 87.5 us (0.69)
  Pallas kernels: 0 us -> 81.4 us
  waiting for transfers between devices: 57.2 us -> 0 us
  starting transfers between devices: 26 us -> 0 us
  blocking collectives: 15 us -> 0 us
  local copies, waits for them, and re-layouts: 14.6 us -> 5.78 us
  matrix products: 8.15 us -> 0 us
  other arithmetic: 4.99 us -> 0 us
    pallas_call x0 -> x1, Pallas kernels: none -> 81.4 us  [per_device(): pl.pallas_call(kernel, out_shape=jax.ShapeDtypeStruct((2, OUT, NT), F32),...]
    all_to_all x2 -> x0, waiting for transfers between devices: 57.2 us -> none  [the longest x1 48.8 us: per_device(): lax.all_to_all(spectra, 'af', split_axis=2, concat_axis=0, tiled=True)]
    all_to_all x2 -> x0, starting transfers between devices: 26 us -> none  [the longest x1 17.9 us: per_device(): lax.all_to_all(spectra, 'af', split_axis=2, concat_axis=0, tiled=True)]
    all_gather x1 -> x0, blocking collectives: 15 us -> none  [per_device(): chosen = lax.all_gather(chosen, 'row', axis=4, tiled=True)]
    dot_general x6 -> x0, matrix products: 8.15 us -> none  [the longest x1 4.25 us: per_device(): jnp.einsum('nc,srn->scr', forward, masked, preferred_element_type=jnp.flo...]
    all_to_all x4 -> x0, local copies, waits for them, and re-layouts: 3.9 us -> none  [the longest x2 3.6 us: per_device(): lax.all_to_all(spectra, 'af', split_axis=2, concat_axis=0, tiled=True)]
    convert_element_type x1 -> x0, local copies, waits for them, and re-layouts: 3.33 us -> none  [per_device(): jnp.einsum('nc,srn->scr', forward, masked, preferred_element_type=jnp.flo...]
    unnamed x8 -> x10, local copies, waits for them, and re-layouts: 2.3 us -> 5.02 us
  transfers between devices with their start and end apart: 2 -> 0, of which waited for: 2 -> 0; matrix products, arithmetic and copies ran while one was open for 2% -> 0% of each run, Pallas kernels for 0% -> 0%
where the time goes in v1:
time: 87.5 us; the launch traced here: 87.2 us
  Pallas kernels  81.4 us (93%)
  local copies, waits for them, and re-layouts  5.78 us (7%)
    pallas_call x1, Pallas kernels, per_device(): pl.pallas_call(kernel, out_shape=jax.ShapeDtypeStruct((2, OUT, NT), F32),...  81.4 us
    unnamed x10, local copies, waits for them, and re-layouts  5.02 us

profile of v1, /device:TPU:1, one launch (start us, length us, event | category | flops | bytes accessed | tf_op | source)
XLA Modules:
  0.0 87.2 jit_solution(5797995921719140448)
XLA Ops:
  0.0 0.0 copy-start
  0.0 1.6 %copy-done = bf16[8,256,512]{2,1,0:T(8,128)(2,1)S(1)} copy-done((bf16[8,256,512]{2,1,0:T(8,128)(2,1)S(1)}, bf16[8,256,512]{2,1,0:T(8,128)(2,1)}, u32[]{:S(2)}) %copy-start) | copy-done | bytes 2097176
  1.6 0.0 copy-start.1
  1.6 0.7 copy-done.1
  2.3 0.0 copy-start.2
  2.3 0.7 copy-done.2
  2.9 0.0 copy-start.3
  2.9 1.0 %copy-done.3 = bf16[512,512]{1,0:T(8,128)(2,1)S(1)} copy-done((bf16[512,512]{1,0:T(8,128)(2,1)S(1)}, bf16[512,512]{1,0:T(8,128)(2,1)}, u32[]{:S(2)}) %copy-start.3) | copy-done | bytes 524312
  4.0 0.0 copy-start.4
  4.0 1.0 %copy-done.4 = bf16[512,512]{1,0:T(8,128)(2,1)S(1)} copy-done((bf16[512,512]{1,0:T(8,128)(2,1)S(1)}, bf16[512,512]{1,0:T(8,128)(2,1)}, u32[]{:S(2)}) %copy-start.4) | copy-done | bytes 524312
  5.0 81.4 %multiples.1 = f32[2,32,512]{2,1,0:T(8,128)S(1)} custom-call(s32[32]{0:T(128)S(1)} %copy-done.2, bf16[8,256,512]{2,1,0:T(8,128)(2,1)S(1)} %copy-done, s32[8,256]{1,0:T(8,128)S(1)} %copy-done.1, bf16[512,512]{1,0:T(8,128)(2,1)S(1)} %copy-done.4, bf16[512,512]{1,0:T(8,128)(2,1)S(1)} %copy-done.3), custom_call_target="tpu_custom_call" | custom-call | flops 2147483648 | bytes 4194304 | tf_op jit(solution)/shard_map/multiples/pallas_call | solution.py:280
  86.4 0.8 copy.6
Async XLA Ops:
  0.0 1.6 %copy-start = (bf16[8,256,512]{2,1,0:T(8,128)(2,1)S(1)}, bf16[8,256,512]{2,1,0:T(8,128)(2,1)}, u32[]{:S(2)}) copy-start(bf16[8,256,512]{2,1,0:T(8,128)(2,1)} %traces_hbm.1) | copy-start | bytes 6291460
  1.6 0.7 copy-start.1
  2.3 0.7 copy-start.2
  2.9 1.0 %copy-start.3 = (bf16[512,512]{1,0:T(8,128)(2,1)S(1)}, bf16[512,512]{1,0:T(8,128)(2,1)}, u32[]{:S(2)}) copy-start(bf16[512,512]{1,0:T(8,128)(2,1)} %constant.5.clone.inv_hbm) | copy-start | bytes 1572868
  4.0 1.0 %copy-start.4 = (bf16[512,512]{1,0:T(8,128)(2,1)S(1)}, bf16[512,512]{1,0:T(8,128)(2,1)}, u32[]{:S(2)}) copy-start(bf16[512,512]{1,0:T(8,128)(2,1)} %constant.4.clone.fwd_hbm) | copy-start | bytes 1572868

commit v2 on v1

v2 whole, which is shorter than its diff:
```python
import functools
import math

import jax
import jax.numpy as jnp
import numpy as np
from jax import lax
from jax.experimental import pallas as pl
from jax.experimental.pallas import tpu as pltpu
from jax.sharding import PartitionSpec as P

MESH = pl.DeviceIdType.MESH
BF, F32, I32 = jnp.bfloat16, jnp.float32, jnp.int32

NX, NY, NZ, NROW = 4, 8, 4, 4
NT, NF, SHOTS, RECV, OUT = 512, 256, 8, 256, 32
BANDS, PER = 32, 8
COMP = 2 * PER
GROUPS = 2
PER_G = PER // GROUPS


def host_tables():
    t = np.arange(NT)[:, None]
    f = np.arange(NF)[None, :]
    ang = (t * f % NT) * (2.0 * math.pi / NT)
    norm = 1.0 / math.sqrt(NT)
    w = np.where(np.arange(NF) == 0, 1.0, 2.0)[:, None]
    cos, sin = np.cos(ang).T, -np.sin(ang).T
    fwd = np.stack([cos.reshape(BANDS, PER, NT), sin.reshape(BANDS, PER, NT)], axis=1) * norm
    inv = np.concatenate([cos * w, sin * w], axis=0) * norm
    as_bf = lambda a: a.astype(np.float32).astype(jnp.bfloat16)
    fwd = fwd.reshape(2 * NF, NT)
    return as_bf(np.concatenate([fwd, fwd[:128]])), as_bf(inv)


def af(x, y, z):
    return (x * NY + y) * NZ + z


def base_of(y):
    return lax.rem(y - 2 + lax.rem(y, 2) + NY, NY)


def iota(shape, dim):
    return lax.broadcasted_iota(I32, shape, dim)


def mm(a, b, dims=((1,), (0,))):
    return lax.dot_general(a, b, (dims, ((), ())), preferred_element_type=F32)


def kernel(
    sel_hbm, traces_hbm, live_hbm, fwd_hbm, inv_hbm, out_ref,
    sel_ref, live_ref, traces, fwd, inv, send, recv, bt, perm, pick, lanes, spread,
    a_own, a_msg, a_in, a_row, p2, stage, r_send, r_recv,
    load_sem, send_sem, recv_sem, own_sem, a_send_sem, a_recv_sem, row_send_sem, row_recv_sem,
    r_send_sem, r_recv_sem, r_own_sem,
):
    a = lax.axis_index("af")
    row = lax.axis_index("row")
    x, y, z = lax.div(a, NY * NZ), lax.rem(lax.div(a, NZ), NY), lax.rem(a, NZ)
    half, zp, zs, odd = lax.div(y, 2), lax.div(z, 2), lax.rem(z, 2), lax.rem(y, 2)
    base = base_of(y)
    xs = [lax.rem(x + i, NX) for i in range(NX)]
    ys = [lax.rem(y + i, NY) for i in range(NY)]
    zz = [lax.rem(z + i, NZ) for i in range(NZ)]
    other = lax.rem(row + 2, NROW)
    cores = (a, row + 1 - 2 * lax.rem(row, 2))
    across = (a, other)
    pair = [z, z + 1 - 2 * zs]
    to_y = [lax.rem(2 * half - 1 + lax.rem(odd + 1 + w, 4) + NY, NY) for w in range(4)]
    from_y = [lax.rem(base + lax.rem(lax.rem(y - base + NY, NY) + w, 4), NY) for w in range(4)]
    homes = [af(x, ys[4 * (u // 2)], zz[2 * (u % 2)]) for u in range(4)]

    fwd_copy = pltpu.make_async_copy(fwd_hbm, fwd, load_sem.at[SHOTS])
    inv_copy = pltpu.make_async_copy(inv_hbm, inv, load_sem.at[SHOTS + 1])
    live_copy = pltpu.make_async_copy(live_hbm, live_ref, load_sem.at[SHOTS + 2])
    sel_copy = pltpu.make_async_copy(sel_hbm, sel_ref, load_sem.at[SHOTS + 3])
    fwd_copy.start()
    live_copy.start()
    loads = [pltpu.make_async_copy(traces_hbm.at[s], traces.at[s], load_sem.at[s]) for s in range(SHOTS)]
    for c in loads:
        c.start()
    inv_copy.start()
    sel_copy.start()

    barrier = pltpu.get_barrier_semaphore()

    for i in range(1, BANDS):
        pl.semaphore_signal(
            barrier, inc=1, device_id=(af(xs[i // 8], from_y[i // 2 % 4], pair[i % 2]), row), device_id_type=MESH
        )
    for u in range(1, 4):
        pl.semaphore_signal(barrier, inc=1, device_id=(homes[u], row), device_id_type=MESH)
    pl.semaphore_signal(barrier, inc=1, device_id=cores, device_id_type=MESH)
    pl.semaphore_signal(barrier, inc=1, device_id=across, device_id_type=MESH)

    fwd_copy.wait()
    live_copy.wait()
    for c in loads:
        c.wait()
    live = live_ref[...].astype(F32)

    def band_of(bx, hy, hz):
        return bx * 8 + lax.rem(hy, 4) * 2 + lax.rem(hz, 2)

    to_slot = [x * 8 + lax.rem(y - base_of(hy) + NY, NY) * 2 + zs for hy in to_y]

    def band_copy(dx, w, dz):
        band, slot = band_of(xs[dx], to_y[w], pair[dz]), to_slot[w]
        return pltpu.make_async_remote_copy(
            src_ref=send.at[band], dst_ref=recv.at[slot], send_sem=send_sem,
            recv_sem=recv_sem.at[slot], device_id=(af(xs[dx], to_y[w], pair[dz]), row), device_id_type=MESH,
        )

    own_band, own_slot = band_of(x, y, z), to_slot[0]
    own_copy = pltpu.make_async_copy(send.at[own_band], recv.at[own_slot], own_sem)

    for i in range(2):
        first = xs[(1 + 2 * i) % NX]
        second = xs[(2 + 2 * i) % NX]
        table = fwd[pl.ds(pl.multiple_of(first * 128, 128), 256), :]
        for s in range(SHOTS):
            spec = (mm(table, traces[s], ((1,), (1,))) * live[s : s + 1, :]).astype(BF)
            spec = spec.reshape(2, 8, COMP, RECV)
            send[pl.ds(first * 8, 8), s] = spec[0]
            send[pl.ds(second * 8, 8), s] = spec[1]
        if i == 0:
            pl.semaphore_wait(barrier, BANDS - 1 + 3 + 2)
        for j in range(16):
            dx, w, dz = (1 + 2 * i + j % 2) % NX, (j // 2 + 1) % 4, (j // 8 + 1) % 2
            if (dx, w, dz) != (0, 0, 0):
                band_copy(dx, w, dz).start()

    own_copy.start()

    ro, co = iota((256, 256), 0), iota((256, 256), 1)
    perm[...] = jnp.where(co == (ro % 16) // 8 * 128 + ro % 8 * 16 + ro // 16, 1.0, 0.0).astype(BF)
    j = iota((1, 512), 1)
    k64 = j % 64
    shot = ((j // 128 * NY + (base + k64 // 16) % NY) * NZ + 2 * zp + k64 // 8 % 2) * SHOTS + k64 % 8
    part = j % 128 // 64
    sel_copy.wait()
    o_at = iota((OUT, 512), 0)
    want = jnp.full((OUT, 512), -1, I32)
    for o in range(OUT):
        want = jnp.where(o_at == o, sel_ref[o], want)
    hit = want == shot
    pick[0:OUT, :] = jnp.where(hit & (part == 0), 1.0, 0.0).astype(BF)
    pick[OUT : 2 * OUT, :] = jnp.where(hit & (part == 1), 1.0, 0.0).astype(BF)
    u = j // 128
    k_here = ((base + 4 * (u // 2) + k64 // 16) % NY * NZ + 2 * ((zp + u) % 2) + k64 // 8 % 2) * 8 + k64 % 8
    from_row = part * RECV + k_here
    lanes[...] = jnp.where(iota((512, 512), 0) == from_row, 1.0, 0.0).astype(BF)
    d_at = iota((128, 512), 0)
    j2 = iota((128, 512), 1)
    spread[...] = jnp.where(j2 % 256 == 2 * d_at + j2 // 256, 1.0, 0.0).astype(BF)
    p2[...] = jnp.zeros_like(p2)

    own_copy.wait()

    @pl.loop(0, NX)
    def _(i):
        sx = lax.rem(x + 2 * NX - 1 - i, NX)
        for q in range(8):
            slot = sx * 8 + q

            @pl.when(slot != own_slot)
            def _():
                pltpu.make_async_remote_copy(
                    src_ref=send.at[0], dst_ref=recv.at[slot], send_sem=send_sem,
                    recv_sem=recv_sem.at[slot], device_id=cores, device_id_type=MESH,
                ).wait_recv()

        for q in range(4):
            block = recv[pl.ds(sx * 8 + q * 2, 2)].reshape(256, RECV)
            turned = mm(perm[...], block).astype(BF).reshape(2, PER, 16, RECV)
            bt[:, sx, 0, q] = turned[0]
            bt[:, sx, 1, q] = turned[1]

    def home_copy(g, v):
        return pltpu.make_async_remote_copy(
            src_ref=a_msg.at[g, v], dst_ref=a_in.at[g, v], send_sem=a_send_sem.at[g, v],
            recv_sem=a_recv_sem.at[g, v], device_id=(homes[v], row), device_id_type=MESH,
        )

    def row_copy(g, slot, to, sem):
        return pltpu.make_async_remote_copy(
            src_ref=a_row.at[slot, g], dst_ref=a_row.at[slot, g], send_sem=row_send_sem.at[g, sem],
            recv_sem=row_recv_sem.at[g, sem], device_id=to, device_id_type=MESH,
        )

    for g in range(GROUPS):
        for f in range(PER_G):
            got = mm(pick[...], bt[g * PER_G + f].reshape(512, RECV)).astype(BF)
            a_own[g, f * OUT : (f + 1) * OUT, 0:RECV] = got[0:OUT]
            a_own[g, f * OUT : (f + 1) * OUT, RECV:] = got[OUT:]
        for v in (3, 2, 1, 0):
            a_msg[g, v] = mm(a_own[g], lanes[:, v * 128 : (v + 1) * 128]).astype(BF)
            if v:
                home_copy(g, v).start()

    to_across = [row_copy(g, row, across, 0) for g in range(GROUPS)]
    to_core = [row_copy(g, row, cores, 1) for g in range(GROUPS)]
    onward = [row_copy(g, other, cores, 2) for g in range(GROUPS)]
    for g in range(GROUPS):
        for v in (1, 2, 3):
            home_copy(g, v).wait()
        a_row[row, g] = a_msg[g, 0] + a_in[g, 1] + a_in[g, 2] + a_in[g, 3]
        to_across[g].start()
        to_core[g].start()
    for g in range(GROUPS):
        to_across[g].wait_recv()
        onward[g].start()

    sign = jnp.where(iota((1, 128), 1) < 64, 1.0, -1.0)
    factor = 1.0 / math.sqrt(NX * NY * NZ * SHOTS)
    for g in range(GROUPS):
        to_core[g].wait_recv()
        onward[g].wait_recv()
        left = []
        for v in range(NROW):
            val = a_row[v, g].astype(F32)
            left.append(((val * sign).astype(BF), pltpu.roll(val, 64, 1).astype(BF)))
        for f in range(PER_G):
            rows = slice(f * OUT, (f + 1) * OUT)
            lhs = jnp.concatenate(
                [jnp.concatenate([left[v][p][rows] for v in range(NROW)], axis=1) for p in range(2)], axis=0
            )
            at = g * PER_G + f
            pred = (mm(lhs, bt[at].reshape(512, RECV)) * factor).astype(BF)
            p2[at, 0:64, 0:RECV] = pred
            p2[at, 64:128, RECV:] = pred

    for f in range(PER):
        stage[pl.ds(f, 128, stride=8), :] = mm(spread[...], p2[f], ((1,), (1,)))
    r_send[...] = stage[...].astype(BF).reshape(128, 8, 128)

    my_slot = (lax.div(y, 4) * 2 + zp) * BANDS + own_band
    own_r = pltpu.make_async_copy(r_send.at[a], r_recv.at[my_slot], r_own_sem)
    own_r.start()

    def back(d):
        pltpu.make_async_remote_copy(
            src_ref=r_send.at[d], dst_ref=r_recv.at[my_slot], send_sem=r_send_sem,
            recv_sem=r_recv_sem, device_id=(d, row), device_id_type=MESH,
        ).start()

    @pl.loop(0, NY)
    def _(i):
        dy = lax.rem(y + 4 + i, NY)
        for j in range(1, 16):
            back(af(xs[j % NX], dy, zz[j // NX]))

        @pl.when(i != 4)
        def _():
            back(af(x, dy, z))

    all_r = pltpu.make_async_remote_copy(
        src_ref=r_send.at[pl.ds(0, 127)], dst_ref=r_recv.at[pl.ds(0, 127)], send_sem=r_send_sem,
        recv_sem=r_recv_sem, device_id=cores, device_id_type=MESH,
    )
    inv_copy.wait()
    own_r.wait()
    all_r.wait_recv()

    total = r_recv[0:32].astype(F32)
    for v in range(1, 4):
        total = total + r_recv[v * 32 : (v + 1) * 32].astype(F32)
    turned = total.reshape(256, 128).T.astype(BF)
    lhs = jnp.concatenate(
        [jnp.concatenate([turned[r * 64 : r * 64 + 32], turned[r * 64 + 32 : r * 64 + 64]], axis=1) for r in range(2)],
        axis=0,
    )
    res = mm(lhs, inv[...])
    for r in range(2):
        out_ref[r] = res[r * 32 : (r + 1) * 32]

    all_r.wait_send()
    for g in range(GROUPS):
        for c in (to_across[g], to_core[g], onward[g]):
            c.wait_send()
    pltpu.make_async_remote_copy(
        src_ref=send.at[pl.ds(0, 31)], dst_ref=recv.at[pl.ds(0, 31)], send_sem=send_sem,
        recv_sem=recv_sem.at[0], device_id=cores, device_id_type=MESH,
    ).wait_send()


def per_device(traces, live, selected):
    fwd, inv = host_tables()
    any_, vmem = pl.BlockSpec(memory_space=pl.ANY), pl.BlockSpec(memory_space=pltpu.VMEM)
    dma = pltpu.SemaphoreType.DMA
    out = pl.pallas_call(
        kernel,
        out_shape=jax.ShapeDtypeStruct((2, OUT, NT), F32),
        in_specs=[any_] * 5,
        out_specs=vmem,
        scratch_shapes=[
            pltpu.SMEM((OUT,), I32),
            pltpu.VMEM((SHOTS, RECV), I32),
            pltpu.VMEM((SHOTS, RECV, NT), BF),
            pltpu.VMEM((2 * NF + 128, NT), BF),
            pltpu.VMEM((2 * NF, NT), BF),
            pltpu.VMEM((BANDS, SHOTS, COMP, RECV), BF),
            pltpu.VMEM((BANDS, SHOTS, COMP, RECV), BF),
            pltpu.VMEM((PER, NX, 2, 4, 16, RECV), BF),
            pltpu.VMEM((256, 256), BF),
            pltpu.VMEM((2 * OUT, 512), BF),
            pltpu.VMEM((512, 512), BF),
            pltpu.VMEM((128, 512), BF),
            pltpu.VMEM((GROUPS, PER_G * OUT, 512), BF),
            pltpu.VMEM((GROUPS, 4, PER_G * OUT, 128), BF),
            pltpu.VMEM((GROUPS, 4, PER_G * OUT, 128), BF),
            pltpu.VMEM((NROW, GROUPS, PER_G * OUT, 128), BF),
            pltpu.VMEM((PER, 128, 512), BF),
            pltpu.VMEM((1024, 128), F32),
            pltpu.VMEM((128, 8, 128), BF),
            pltpu.VMEM((128, 8, 128), BF),
            dma((SHOTS + 4,)), dma, dma((BANDS,)), dma,
            dma((GROUPS, 4)), dma((GROUPS, 4)), dma((GROUPS, 3)), dma((GROUPS, 3)),
            dma, dma, dma,
        ],
        compiler_params=pltpu.CompilerParams(
            collective_id=0, has_side_effects=True, vmem_limit_bytes=60 << 20
        ),
        cost_estimate=pl.CostEstimate(flops=2 << 30, bytes_accessed=4 << 20, transcendentals=0),
        name="multiples",
    )(selected, traces, live, jnp.asarray(fwd), jnp.asarray(inv))
    return out.transpose(1, 0, 2)[:, None]


def solution(mesh):
    in_specs = (P("af", "row", None), P("af", "row"), P())
    out_specs = P(None, "row", "af", None)
    return jax.shard_map(per_device, mesh=mesh, in_specs=in_specs, out_specs=out_specs, check_vma=False)
```

time: 87.5 us -> 80.8 us (0.923)
  local copies, waits for them, and re-layouts: 5.78 us -> 1.66 us
  Pallas kernels: 81.4 us -> 79 us
    unnamed x10 -> x0, local copies, waits for them, and re-layouts: 5.02 us -> none
    pallas_call x1, Pallas kernels: 81.4 us -> 79 us  [per_device(): pl.pallas_call(kernel, out_shape=jax.ShapeDtypeStruct((2, OUT, NT), F32),...]
    broadcast_in_dim x1, local copies, waits for them, and re-layouts: 0.76 us -> 1.66 us  [per_device(): return out.transpose(1, 0, 2)[:, None]]
where the time goes in v2:
time: 80.8 us; the launch traced here: 80.7 us
  Pallas kernels  79 us (98%)
  local copies, waits for them, and re-layouts  1.66 us (2%)
    pallas_call x1, Pallas kernels, per_device(): pl.pallas_call(kernel, out_shape=jax.ShapeDtypeStruct((2, OUT, NT), F32),...  79 us
    broadcast_in_dim x1, local copies, waits for them, and re-layouts, per_device(): return out.transpose(1, 0, 2)[:, None]  1.66 us

profile of v2, /device:TPU:1, one launch (start us, length us, event | category | flops | bytes accessed | tf_op | source)
XLA Modules:
  0.0 80.7 jit_solution(12187462670743686349)
XLA Ops:
  0.0 79.0 %multiples.1 = f32[2,32,512]{2,1,0:T(8,128)} custom-call(s32[32]{0:T(128)} %sel_hbm.1, bf16[8,256,512]{2,1,0:T(8,128)(2,1)} %traces_hbm.1, s32[8,256]{1,0:T(8,128)} %live_hbm.1, bf16[640,512]{1,0:T(8,128)(2,1)} %constant.4.clone.fwd_hbm, bf16[512,512]{1,0:T(8,128)(2,1)} %constant.5.clone.inv_hbm), custom_call_target="tpu_custom_call" | custom-call | flops 2147483648 | bytes 4194304 | tf_op jit(solution)/shard_map/multiples/pallas_call | solution.py:294
  79.0 1.7 %copy.6 = f32[32,1,2,512]{3,2,1,0:T(2,128)} copy(f32[32,1,2,512]{3,0,2,1:T(8,128)} %bitcast.3) | data formatting | bytes 262144 | tf_op jit(solution)/shard_map/broadcast_in_dim | solution.py:330

commit v3 on v2

--- a/solution.py
+++ b/solution.py
@@ -51,12 +51,17 @@
 
 
 def kernel(
-    sel_hbm, traces_hbm, live_hbm, fwd_hbm, inv_hbm, out_ref,
+    phases, sel_hbm, traces_hbm, live_hbm, fwd_hbm, inv_hbm, out_ref,
     sel_ref, live_ref, traces, fwd, inv, send, recv, bt, perm, pick, lanes, spread,
     a_own, a_msg, a_in, a_row, p2, stage, r_send, r_recv,
     load_sem, send_sem, recv_sem, own_sem, a_send_sem, a_recv_sem, row_send_sem, row_recv_sem,
     r_send_sem, r_recv_sem, r_own_sem,
 ):
+    per_phase = SHOTS // phases
+    joined = 16 // per_phase
+    blocks = 8 // joined
+    run = 64 // phases
+
     a = lax.axis_index("af")
     row = lax.axis_index("row")
     x, y, z = lax.div(a, NY * NZ), lax.rem(lax.div(a, NZ), NY), lax.rem(a, NZ)
@@ -77,13 +82,13 @@
     inv_copy = pltpu.make_async_copy(inv_hbm, inv, load_sem.at[SHOTS + 1])
     live_copy = pltpu.make_async_copy(live_hbm, live_ref, load_sem.at[SHOTS + 2])
     sel_copy = pltpu.make_async_copy(sel_hbm, sel_ref, load_sem.at[SHOTS + 3])
+    sel_copy.start()
     fwd_copy.start()
     live_copy.start()
     loads = [pltpu.make_async_copy(traces_hbm.at[s], traces.at[s], load_sem.at[s]) for s in range(SHOTS)]
     for c in loads:
         c.start()
     inv_copy.start()
-    sel_copy.start()
 
     barrier = pltpu.get_barrier_semaphore()
 
@@ -96,88 +101,127 @@
     pl.semaphore_signal(barrier, inc=1, device_id=cores, device_id_type=MESH)
     pl.semaphore_signal(barrier, inc=1, device_id=across, device_id_type=MESH)
 
+    sel_copy.wait()
+    chosen = [sel_ref[o] - a * SHOTS for o in range(OUT)]
+    flag = [sum((c == s).astype(I32) for c in chosen) for s in range(SHOTS)]
+    count = sum(flag)
+    place, ahead = [], 0
+    for s in range(SHOTS):
+        place.append(jnp.where(flag[s] > 0, ahead, count + s - ahead))
+        ahead = ahead + flag[s]
+    shot_at = [sum(jnp.where(place[s] == n, s, 0) for s in range(SHOTS)) for n in range(SHOTS)]
+
     fwd_copy.wait()
     live_copy.wait()
     for c in loads:
         c.wait()
-    live = live_ref[...].astype(F32)
 
     def band_of(bx, hy, hz):
         return bx * 8 + lax.rem(hy, 4) * 2 + lax.rem(hz, 2)
 
     to_slot = [x * 8 + lax.rem(y - base_of(hy) + NY, NY) * 2 + zs for hy in to_y]
 
-    def band_copy(dx, w, dz):
+    def band_copy(ph, dx, w, dz):
         band, slot = band_of(xs[dx], to_y[w], pair[dz]), to_slot[w]
         return pltpu.make_async_remote_copy(
-            src_ref=send.at[band], dst_ref=recv.at[slot], send_sem=send_sem,
-            recv_sem=recv_sem.at[slot], device_id=(af(xs[dx], to_y[w], pair[dz]), row), device_id_type=MESH,
+            src_ref=send.at[ph, band], dst_ref=recv.at[ph, slot],
+            send_sem=send_sem.at[(dx * 4 + w) * 2 + dz if ph < phases - 1 else 0],
+            recv_sem=recv_sem.at[ph, slot], device_id=(af(xs[dx], to_y[w], pair[dz]), row), device_id_type=MESH,
         )
 
     own_band, own_slot = band_of(x, y, z), to_slot[0]
-    own_copy = pltpu.make_async_copy(send.at[own_band], recv.at[own_slot], own_sem)
-
-    for i in range(2):
-        first = xs[(1 + 2 * i) % NX]
-        second = xs[(2 + 2 * i) % NX]
-        table = fwd[pl.ds(pl.multiple_of(first * 128, 128), 256), :]
-        for s in range(SHOTS):
-            spec = (mm(table, traces[s], ((1,), (1,))) * live[s : s + 1, :]).astype(BF)
-            spec = spec.reshape(2, 8, COMP, RECV)
-            send[pl.ds(first * 8, 8), s] = spec[0]
-            send[pl.ds(second * 8, 8), s] = spec[1]
-        if i == 0:
-            pl.semaphore_wait(barrier, BANDS - 1 + 3 + 2)
-        for j in range(16):
-            dx, w, dz = (1 + 2 * i + j % 2) % NX, (j // 2 + 1) % 4, (j // 8 + 1) % 2
-            if (dx, w, dz) != (0, 0, 0):
-                band_copy(dx, w, dz).start()
-
-    own_copy.start()
+    own_copies = [
+        pltpu.make_async_copy(send.at[ph, own_band], recv.at[ph, own_slot], own_sem.at[ph]) for ph in range(phases)
+    ]
+    order = [
+        [((1 + 2 * i + j % 2) % NX, (j // 2 + 1) % 4, (j // 8 + 1) % 2) for j in range(16)] for i in range(2)
+    ]
+    order = [[t for t in part if t != (0, 0, 0)] for part in order]
+
+    for ph in range(phases):
+        for i in range(2):
+            first = xs[(1 + 2 * i) % NX]
+            second = xs[(2 + 2 * i) % NX]
+            table = fwd[pl.ds(pl.multiple_of(first * 128, 128), 256), :]
+            for n in range(per_phase):
+                shot = shot_at[ph * per_phase + n]
+                spec = mm(table, traces[shot], ((1,), (1,))) * live_ref[pl.ds(shot, 1), :].astype(F32)
+                spec = spec.astype(BF).reshape(2, 8, COMP, RECV)
+                send[ph, pl.ds(first * 8, 8), n] = spec[0]
+                send[ph, pl.ds(second * 8, 8), n] = spec[1]
+            if ph == 0:
+                if i == 0:
+                    pl.semaphore_wait(barrier, BANDS - 1 + 3 + 2)
+                for t in order[i]:
+                    band_copy(0, *t).start()
+        own_copies[ph].start()
 
     ro, co = iota((256, 256), 0), iota((256, 256), 1)
-    perm[...] = jnp.where(co == (ro % 16) // 8 * 128 + ro % 8 * 16 + ro // 16, 1.0, 0.0).astype(BF)
-    j = iota((1, 512), 1)
-    k64 = j % 64
-    shot = ((j // 128 * NY + (base + k64 // 16) % NY) * NZ + 2 * zp + k64 // 8 % 2) * SHOTS + k64 % 8
-    part = j % 128 // 64
-    sel_copy.wait()
-    o_at = iota((OUT, 512), 0)
-    want = jnp.full((OUT, 512), -1, I32)
+    perm[...] = jnp.where(co == ro % 16 * 16 + ro // 16, 1.0, 0.0).astype(BF)
+    col = jnp.full((OUT, 128), -1, I32)
+    line = jnp.full((1, 128), -1, I32)
     for o in range(OUT):
-        want = jnp.where(o_at == o, sel_ref[o], want)
-    hit = want == shot
+        col = jnp.where(iota((OUT, 128), 0) == o, sel_ref[o], col)
+        line = jnp.where(iota((1, 128), 1) == o, sel_ref[o], line)
+    before = (line // SHOTS == col // SHOTS) & (line < col) & (iota((OUT, 128), 1) < OUT)
+    rank = jnp.sum(jnp.where(before, 1.0, 0.0), axis=1, keepdims=True).astype(I32)
+    want = col[:, 0:1] // SHOTS * SHOTS + rank
+    j = iota((1, 512 // phases), 1)
+    k = j % run
+    src, place_k = k // per_phase, k % per_phase
+    part = j // run % 2
+    device = (j // (2 * run) * NY + (base + src // 2) % NY) * NZ + 2 * zp + src % 2
+    hit = want == device * SHOTS + place_k
     pick[0:OUT, :] = jnp.where(hit & (part == 0), 1.0, 0.0).astype(BF)
     pick[OUT : 2 * OUT, :] = jnp.where(hit & (part == 1), 1.0, 0.0).astype(BF)
-    u = j // 128
-    k_here = ((base + 4 * (u // 2) + k64 // 16) % NY * NZ + 2 * ((zp + u) % 2) + k64 // 8 % 2) * 8 + k64 % 8
-    from_row = part * RECV + k_here
-    lanes[...] = jnp.where(iota((512, 512), 0) == from_row, 1.0, 0.0).astype(BF)
+    r_at = iota((256, 128), 0)
+    here = jnp.where((row * RECV + r_at == line) & (iota((256, 128), 1) < OUT), 1.0, 0.0)
+    same = ro // SHOTS == co // SHOTS
+    ahead_of = mm(jnp.where(same & (co < ro), 1.0, 0.0).astype(BF), here.astype(BF))
+    all_of = mm(jnp.where(same, 1.0, 0.0).astype(BF), here.astype(BF))
+    total_of = lambda v: jnp.sum(v, axis=1, keepdims=True).astype(I32)
+    n_here, n_ahead, n_all = total_of(here), total_of(ahead_of), total_of(all_of)
+    r1 = iota((256, 1), 0)
+    at = jnp.where(n_here > 0, n_ahead, n_all + r1 % SHOTS - n_ahead)
+    ry, rz = (r1 // (NZ * SHOTS) - base + NY) % NY, r1 // SHOTS % NZ
+    u = ry // 4 * 2 + jnp.where(rz // 2 == zp, 0, 1)
+    to = u * 128 + at // per_phase * (2 * run) + (ry % 4 * 2 + rz % 2) * per_phase + at % per_phase
+    for p in range(2):
+        lanes[p * 256 : (p + 1) * 256, :] = jnp.where(iota((256, 512), 1) == to + p * run, 1.0, 0.0).astype(BF)
     d_at = iota((128, 512), 0)
     j2 = iota((128, 512), 1)
     spread[...] = jnp.where(j2 % 256 == 2 * d_at + j2 // 256, 1.0, 0.0).astype(BF)
     p2[...] = jnp.zeros_like(p2)
 
-    own_copy.wait()
-
-    @pl.loop(0, NX)
-    def _(i):
-        sx = lax.rem(x + 2 * NX - 1 - i, NX)
-        for q in range(8):
-            slot = sx * 8 + q
-
-            @pl.when(slot != own_slot)
-            def _():
-                pltpu.make_async_remote_copy(
-                    src_ref=send.at[0], dst_ref=recv.at[slot], send_sem=send_sem,
-                    recv_sem=recv_sem.at[slot], device_id=cores, device_id_type=MESH,
-                ).wait_recv()
-
-        for q in range(4):
-            block = recv[pl.ds(sx * 8 + q * 2, 2)].reshape(256, RECV)
-            turned = mm(perm[...], block).astype(BF).reshape(2, PER, 16, RECV)
-            bt[:, sx, 0, q] = turned[0]
-            bt[:, sx, 1, q] = turned[1]
+    for i in range(2):
+        for t in order[i]:
+            if phases == 2:
+                band_copy(0, *t).wait_send()
+                band_copy(1, *t).start()
+
+    def arrive(ph, start, stop):
+        @pl.loop(start, stop)
+        def _(i):
+            sx = lax.rem(x + 2 * NX - 1 - i, NX)
+            for q in range(8):
+                slot = sx * 8 + q
+
+                @pl.when(slot != own_slot)
+                def _():
+                    pltpu.make_async_remote_copy(
+                        src_ref=send.at[ph, 0], dst_ref=recv.at[ph, slot], send_sem=send_sem.at[0],
+                        recv_sem=recv_sem.at[ph, slot], device_id=cores, device_id_type=MESH,
+                    ).wait_recv()
+
+            for q in range(blocks):
+                block = recv[ph, pl.ds(sx * 8 + q * joined, joined)].reshape(256, RECV)
+                turned = mm(perm[...], block).astype(BF).reshape(2, PER, 16, RECV)
+                bt[:, sx, ph, 0, q] = turned[0]
+                bt[:, sx, ph, 1, q] = turned[1]
+
+    for c in own_copies:
+        c.wait()
+    arrive(0, 0, NX)
 
     def home_copy(g, v):
         return pltpu.make_async_remote_copy(
@@ -193,7 +237,7 @@
 
     for g in range(GROUPS):
         for f in range(PER_G):
-            got = mm(pick[...], bt[g * PER_G + f].reshape(512, RECV)).astype(BF)
+            got = mm(pick[...], bt[g * PER_G + f, :, 0].reshape(512 // phases, RECV)).astype(BF)
             a_own[g, f * OUT : (f + 1) * OUT, 0:RECV] = got[0:OUT]
             a_own[g, f * OUT : (f + 1) * OUT, RECV:] = got[OUT:]
         for v in (3, 2, 1, 0):
@@ -210,11 +254,16 @@
         a_row[row, g] = a_msg[g, 0] + a_in[g, 1] + a_in[g, 2] + a_in[g, 3]
         to_across[g].start()
         to_core[g].start()
+    if phases == 2:
+        arrive(1, 0, 2)
     for g in range(GROUPS):
         to_across[g].wait_recv()
         onward[g].start()
-
-    sign = jnp.where(iota((1, 128), 1) < 64, 1.0, -1.0)
+    if phases == 2:
+        arrive(1, 2, NX)
+
+    imag = iota((1, 128), 1) // run % 2 == 1
+    sign = jnp.where(imag, -1.0, 1.0)
     factor = 1.0 / math.sqrt(NX * NY * NZ * SHOTS)
     for g in range(GROUPS):
         to_core[g].wait_recv()
@@ -222,7 +271,8 @@
         left = []
         for v in range(NROW):
             val = a_row[v, g].astype(F32)
-            left.append(((val * sign).astype(BF), pltpu.roll(val, 64, 1).astype(BF)))
+            swapped = jnp.where(imag, pltpu.roll(val, run, 1), pltpu.roll(val, 128 - run, 1))
+            left.append(((val * sign).astype(BF), swapped.astype(BF)))
         for f in range(PER_G):
             rows = slice(f * OUT, (f + 1) * OUT)
             lhs = jnp.concatenate(
@@ -282,8 +332,8 @@
         for c in (to_across[g], to_core[g], onward[g]):
             c.wait_send()
     pltpu.make_async_remote_copy(
-        src_ref=send.at[pl.ds(0, 31)], dst_ref=recv.at[pl.ds(0, 31)], send_sem=send_sem,
-        recv_sem=recv_sem.at[0], device_id=cores, device_id_type=MESH,
+        src_ref=send.at[phases - 1, pl.ds(0, 31)], dst_ref=recv.at[phases - 1, pl.ds(0, 31)],
+        send_sem=send_sem.at[0], recv_sem=recv_sem.at[0, 0], device_id=cores, device_id_type=MESH,
     ).wait_send()
 
 
@@ -291,42 +341,49 @@
     fwd, inv = host_tables()
     any_, vmem = pl.BlockSpec(memory_space=pl.ANY), pl.BlockSpec(memory_space=pltpu.VMEM)
     dma = pltpu.SemaphoreType.DMA
-    out = pl.pallas_call(
-        kernel,
-        out_shape=jax.ShapeDtypeStruct((2, OUT, NT), F32),
-        in_specs=[any_] * 5,
-        out_specs=vmem,
-        scratch_shapes=[
-            pltpu.SMEM((OUT,), I32),
-            pltpu.VMEM((SHOTS, RECV), I32),
-            pltpu.VMEM((SHOTS, RECV, NT), BF),
-            pltpu.VMEM((2 * NF + 128, NT), BF),
-            pltpu.VMEM((2 * NF, NT), BF),
-            pltpu.VMEM((BANDS, SHOTS, COMP, RECV), BF),
-            pltpu.VMEM((BANDS, SHOTS, COMP, RECV), BF),
-            pltpu.VMEM((PER, NX, 2, 4, 16, RECV), BF),
-            pltpu.VMEM((256, 256), BF),
-            pltpu.VMEM((2 * OUT, 512), BF),
-            pltpu.VMEM((512, 512), BF),
-            pltpu.VMEM((128, 512), BF),
-            pltpu.VMEM((GROUPS, PER_G * OUT, 512), BF),
-            pltpu.VMEM((GROUPS, 4, PER_G * OUT, 128), BF),
-            pltpu.VMEM((GROUPS, 4, PER_G * OUT, 128), BF),
-            pltpu.VMEM((NROW, GROUPS, PER_G * OUT, 128), BF),
-            pltpu.VMEM((PER, 128, 512), BF),
-            pltpu.VMEM((1024, 128), F32),
-            pltpu.VMEM((128, 8, 128), BF),
-            pltpu.VMEM((128, 8, 128), BF),
-            dma((SHOTS + 4,)), dma, dma((BANDS,)), dma,
-            dma((GROUPS, 4)), dma((GROUPS, 4)), dma((GROUPS, 3)), dma((GROUPS, 3)),
-            dma, dma, dma,
-        ],
-        compiler_params=pltpu.CompilerParams(
-            collective_id=0, has_side_effects=True, vmem_limit_bytes=60 << 20
-        ),
-        cost_estimate=pl.CostEstimate(flops=2 << 30, bytes_accessed=4 << 20, transcendentals=0),
-        name="multiples",
-    )(selected, traces, live, jnp.asarray(fwd), jnp.asarray(inv))
+
+    def call(phases):
+        per_phase, blocks = SHOTS // phases, SHOTS * SHOTS // 16 // phases
+        return pl.pallas_call(
+            functools.partial(kernel, phases),
+            out_shape=jax.ShapeDtypeStruct((2, OUT, NT), F32),
+            in_specs=[any_] * 5,
+            out_specs=vmem,
+            scratch_shapes=[
+                pltpu.SMEM((OUT,), I32),
+                pltpu.VMEM((SHOTS, RECV), I32),
+                pltpu.VMEM((SHOTS, RECV, NT), BF),
+                pltpu.VMEM((2 * NF + 128, NT), BF),
+                pltpu.VMEM((2 * NF, NT), BF),
+                pltpu.VMEM((phases, BANDS, per_phase, COMP, RECV), BF),
+                pltpu.VMEM((phases, BANDS, per_phase, COMP, RECV), BF),
+                pltpu.VMEM((PER, NX, phases, 2, blocks, 16, RECV), BF),
+                pltpu.VMEM((256, 256), BF),
+                pltpu.VMEM((2 * OUT, 512 // phases), BF),
+                pltpu.VMEM((512, 512), BF),
+                pltpu.VMEM((128, 512), BF),
+                pltpu.VMEM((GROUPS, PER_G * OUT, 512), BF),
+                pltpu.VMEM((GROUPS, 4, PER_G * OUT, 128), BF),
+                pltpu.VMEM((GROUPS, 4, PER_G * OUT, 128), BF),
+                pltpu.VMEM((NROW, GROUPS, PER_G * OUT, 128), BF),
+                pltpu.VMEM((PER, 128, 512), BF),
+                pltpu.VMEM((1024, 128), F32),
+                pltpu.VMEM((128, 8, 128), BF),
+                pltpu.VMEM((128, 8, 128), BF),
+                dma((SHOTS + 4,)), dma((BANDS,)), dma((phases, BANDS)), dma((phases,)),
+                dma((GROUPS, 4)), dma((GROUPS, 4)), dma((GROUPS, 3)), dma((GROUPS, 3)),
+                dma, dma, dma,
+            ],
+            compiler_params=pltpu.CompilerParams(
+                collective_id=phases, has_side_effects=True, vmem_limit_bytes=60 << 20
+            ),
+            cost_estimate=pl.CostEstimate(flops=2 << 30, bytes_accessed=4 << 20, transcendentals=0),
+            name="multiples",
+        )(selected, traces, live, jnp.asarray(fwd), jnp.asarray(inv))
+
+    owner = selected // SHOTS
+    most = jnp.max(jnp.sum((owner[:, None] == owner[None, :]).astype(I32), axis=1))
+    out = lax.cond(most <= SHOTS // 2, lambda: call(2), lambda: call(1))
     return out.transpose(1, 0, 2)[:, None]
 
 

time: 80.8 us -> 76.3 us (0.944)
  Pallas kernels: 79 us -> 73.3 us
  other arithmetic: 0 us -> 1.48 us
  local copies, waits for them, and re-layouts: 1.66 us -> 0.76 us
    pallas_call x1, Pallas kernels: 79 us -> 73.3 us  [call(): pl.pallas_call(functools.partial(kernel, phases), out_shape=jax.ShapeDtyp...]
    broadcast_in_dim x1 -> x0, local copies, waits for them, and re-layouts: 1.66 us -> none  [per_device(): return out.transpose(1, 0, 2)[:, None]]
where the time goes in v3:
time: 76.3 us; the launch traced here: 76.2 us
  Pallas kernels  73.3 us (96%)
  other arithmetic  1.48 us (2%)
    pallas_call x1, Pallas kernels, call(): pl.pallas_call(functools.partial(kernel, phases), out_shape=jax.ShapeDtyp...  73.3 us

profile of v3, /device:TPU:1, one launch (start us, length us, event | category | flops | bytes accessed | tf_op | source)
XLA Modules:
  0.0 76.2 jit_solution(505476502075522612)
XLA Ops:
  0.0 0.7 and_select_fusion
  0.7 0.2 convert_reduce_fusion
  0.8 0.6 reduce_max.9
  2.1 73.3 %conditional.1 = (f32[2,32,512]{2,1,0:T(8,128)S(1)}) conditional(s32[]{:T(128)} %convert_element_type.7, (s32[32]{0:T(128)}, bf16[8,256,512]{2,1,0:T(8,128)(2,1)}, s32[8,256]{1,0:T(8,128)}, bf16[640,512]{1,0:T(8,128)(2,1)}, bf16[512,512]{1,0:T(8,128)(2,1)}) %tuple.11, (s32[32]{0:T(128)}, bf16[8,256,512]{2,1,0:T(8,128)(2,1)}, s32[8,256]{1,0:T(8,128)}, ...), branch_computations={%region_2.3_spmd, %region_3.4_spmd} | conditional | flops 2147483648 | bytes 4194312 | solution.py:386
  2.2 73.3 %multiples.3 = f32[2,32,512]{2,1,0:T(8,128)S(1)} custom-call(s32[32]{0:T(128)} %get-tuple-element.33.sel_hbm, bf16[8,256,512]{2,1,0:T(8,128)(2,1)} %get-tuple-element.34.traces_hbm, s32[8,256]{1,0:T(8,128)} %get-tuple-element.35.live_hbm, bf16[640,512]{1,0:T(8,128)(2,1)} %get-tuple-element.36.fwd_hbm, bf16[512,512]{1,0:T(8,128)(2,1)} %get-tuple-element.37.inv_hbm), custom_call_target="tpu_custom_call" | custom-call | flops 2147483648 | bytes 4194304 | tf_op jit(solution)/shard_map/cond/branch_1_fun/multiples/pallas_call | solution.py:347
  75.4 0.8 copy.9

commit v4 on v3

--- a/solution.py
+++ b/solution.py
@@ -18,6 +18,7 @@
 COMP = 2 * PER
 GROUPS = 2
 PER_G = PER // GROUPS
+METER = (8, 18, 31)
 
 
 def host_tables():
@@ -193,11 +194,12 @@
     spread[...] = jnp.where(j2 % 256 == 2 * d_at + j2 // 256, 1.0, 0.0).astype(BF)
     p2[...] = jnp.zeros_like(p2)
 
-    for i in range(2):
-        for t in order[i]:
-            if phases == 2:
-                band_copy(0, *t).wait_send()
-                band_copy(1, *t).start()
+    def second_phase(start, stop):
+        for t in (order[0] + order[1])[start:stop] if phases == 2 else ():
+            band_copy(0, *t).wait_send()
+            band_copy(1, *t).start()
+
+    second_phase(0, METER[0])
 
     def arrive(ph, start, stop):
         @pl.loop(start, stop)
@@ -245,6 +247,8 @@
             if v:
                 home_copy(g, v).start()
 
+    second_phase(METER[0], METER[1])
+
     to_across = [row_copy(g, row, across, 0) for g in range(GROUPS)]
     to_core = [row_copy(g, row, cores, 1) for g in range(GROUPS)]
     onward = [row_copy(g, other, cores, 2) for g in range(GROUPS)]
@@ -254,11 +258,13 @@
         a_row[row, g] = a_msg[g, 0] + a_in[g, 1] + a_in[g, 2] + a_in[g, 3]
         to_across[g].start()
         to_core[g].start()
+    second_phase(METER[1], METER[2])
     if phases == 2:
         arrive(1, 0, 2)
     for g in range(GROUPS):
         to_across[g].wait_recv()
         onward[g].start()
+    second_phase(METER[2], BANDS)
     if phases == 2:
         arrive(1, 2, NX)
 

time: 76.3 us -> 68.5 us (0.90)
  Pallas kernels: 73.3 us -> 65.4 us
    pallas_call x1, Pallas kernels: 73.3 us -> 65.4 us  [call(): pl.pallas_call(functools.partial(kernel, phases), out_shape=jax.ShapeDtyp...]
where the time goes in v4:
time: 68.5 us; the launch traced here: 68.3 us
  Pallas kernels  65.4 us (95%)
  other arithmetic  1.48 us (2%)
  local copies, waits for them, and re-layouts  0.76 us (1%)
    pallas_call x1, Pallas kernels, call(): pl.pallas_call(functools.partial(kernel, phases), out_shape=jax.ShapeDtyp...  65.4 us

profile of v4, /device:TPU:1, one launch (start us, length us, event | category | flops | bytes accessed | tf_op | source)
XLA Modules:
  0.0 68.3 jit_solution(5013892095306145157)
XLA Ops:
  0.0 0.7 and_select_fusion
  0.7 0.2 convert_reduce_fusion
  0.8 0.6 reduce_max.9
  2.1 65.4 %conditional.1 = (f32[2,32,512]{2,1,0:T(8,128)S(1)}) conditional(s32[]{:T(128)} %convert_element_type.7, (s32[32]{0:T(128)}, bf16[8,256,512]{2,1,0:T(8,128)(2,1)}, s32[8,256]{1,0:T(8,128)}, bf16[640,512]{1,0:T(8,128)(2,1)}, bf16[512,512]{1,0:T(8,128)(2,1)}) %tuple.11, (s32[32]{0:T(128)}, bf16[8,256,512]{2,1,0:T(8,128)(2,1)}, s32[8,256]{1,0:T(8,128)}, ...), branch_computations={%region_2.3_spmd, %region_3.4_spmd} | conditional | flops 2147483648 | bytes 4194312 | solution.py:392
  2.2 65.4 %multiples.3 = f32[2,32,512]{2,1,0:T(8,128)S(1)} custom-call(s32[32]{0:T(128)} %get-tuple-element.33.sel_hbm, bf16[8,256,512]{2,1,0:T(8,128)(2,1)} %get-tuple-element.34.traces_hbm, s32[8,256]{1,0:T(8,128)} %get-tuple-element.35.live_hbm, bf16[640,512]{1,0:T(8,128)(2,1)} %get-tuple-element.36.fwd_hbm, bf16[512,512]{1,0:T(8,128)(2,1)} %get-tuple-element.37.inv_hbm), custom_call_target="tpu_custom_call" | custom-call | flops 2147483648 | bytes 4194304 | tf_op jit(solution)/shard_map/cond/branch_1_fun/multiples/pallas_call | solution.py:353
  67.6 0.8 %copy.9 = f32[2,32,512]{2,0,1:T(2,128)} copy(f32[2,32,512]{2,1,0:T(8,128)S(1)} %get-tuple-element.38) | data formatting | bytes 262144 | tf_op jit(solution)/shard_map/cond | solution.py:392

commit v5 on v4

v5 whole, which is shorter than its diff:
```python
import functools
import math

import jax
import jax.numpy as jnp
import numpy as np
from jax import lax
from jax.experimental import pallas as pl
from jax.experimental.pallas import tpu as pltpu
from jax.sharding import PartitionSpec as P

MESH = pl.DeviceIdType.MESH
BF, F32, I32 = jnp.bfloat16, jnp.float32, jnp.int32

NX, NY, NZ, NROW = 4, 8, 4, 4
NT, NF, SHOTS, RECV, OUT = 512, 256, 8, 256, 32
BANDS, PER = 32, 8
COMP = 2 * PER
EARLY, CAP = 4, 16
METER = (0, 31, 0)


def host_tables():
    t = np.arange(NT)[:, None]
    f = np.arange(NF)[None, :]
    ang = (t * f % NT) * (2.0 * math.pi / NT)
    norm = 1.0 / math.sqrt(NT)
    w = np.where(np.arange(NF) == 0, 1.0, 2.0)[:, None]
    cos, sin = np.cos(ang).T, -np.sin(ang).T
    fwd = np.stack([cos.reshape(BANDS, PER, NT), sin.reshape(BANDS, PER, NT)], axis=1) * norm
    inv = np.concatenate([cos * w, sin * w], axis=0) * norm
    as_bf = lambda a: a.astype(np.float32).astype(jnp.bfloat16)
    fwd = fwd.reshape(2 * NF, NT)
    return as_bf(np.concatenate([fwd, fwd[:128]])), as_bf(inv)


def af(x, y, z):
    return (x * NY + y) * NZ + z


def base_of(y):
    return lax.rem(y - 2 + lax.rem(y, 2) + NY, NY)


def iota(shape, dim):
    return lax.broadcasted_iota(I32, shape, dim)


def mm(a, b, dims=((1,), (0,))):
    return lax.dot_general(a, b, (dims, ((), ())), preferred_element_type=F32)


def kernel(
    early, cap, sel_hbm, traces_hbm, live_hbm, fwd_hbm, inv_hbm, out_ref,
    sel_ref, src_ref, place_ref, group_ref, live_ref, traces, fwd, inv, send_a, send_b, recv_a, recv_b,
    bt, turn, pack, picked, lanes, expand, spread, a_own, a_msg, a_in, a_row, p2, stage, r_send, r_recv,
    load_sem, send_sem, recv_sem, own_sem, a_send_sem, a_recv_sem, row_send_sem, row_recv_sem,
    r_send_sem, r_recv_sem, r_own_sem, homes_sem,
):
    phases = 1 if early == SHOTS else 2
    sends, recvs = (send_a, send_b), (recv_a, recv_b)
    parts = ((0, early), (early, SHOTS))

    a = lax.axis_index("af")
    row = lax.axis_index("row")
    x, y, z = lax.div(a, NY * NZ), lax.rem(lax.div(a, NZ), NY), lax.rem(a, NZ)
    half, zp, zs, odd = lax.div(y, 2), lax.div(z, 2), lax.rem(z, 2), lax.rem(y, 2)
    base = base_of(y)
    xs = [lax.rem(x + i, NX) for i in range(NX)]
    ys = [lax.rem(y + i, NY) for i in range(NY)]
    zz = [lax.rem(z + i, NZ) for i in range(NZ)]
    other = lax.rem(row + 2, NROW)
    cores = (a, row + 1 - 2 * lax.rem(row, 2))
    pair = [z, z + 1 - 2 * zs]
    to_y = [lax.rem(2 * half - 1 + lax.rem(odd + 1 + w, 4) + NY, NY) for w in range(4)]
    from_y = [lax.rem(base + lax.rem(lax.rem(y - base + NY, NY) + w, 4), NY) for w in range(4)]
    homes = [af(x, ys[4 * (u // 2)], zz[2 * (u % 2)]) for u in range(4)]

    fwd_copy = pltpu.make_async_copy(fwd_hbm, fwd, load_sem.at[SHOTS])
    inv_copy = pltpu.make_async_copy(inv_hbm, inv, load_sem.at[SHOTS + 1])
    live_copy = pltpu.make_async_copy(live_hbm, live_ref, load_sem.at[SHOTS + 2])
    sel_copy = pltpu.make_async_copy(sel_hbm, sel_ref, load_sem.at[SHOTS + 3])
    sel_copy.start()
    fwd_copy.start()
    live_copy.start()
    loads = [pltpu.make_async_copy(traces_hbm.at[s], traces.at[s], load_sem.at[s]) for s in range(SHOTS)]
    for c in loads:
        c.start()
    inv_copy.start()

    barrier = pltpu.get_barrier_semaphore()

    pl.semaphore_signal(barrier, inc=1, device_id=(a, other), device_id_type=MESH)
    for u in range(1, 4):
        pl.semaphore_signal(barrier, inc=1, device_id=(homes[u], row), device_id_type=MESH)
    pl.semaphore_signal(barrier, inc=1, device_id=cores, device_id_type=MESH)
    for i in range(1, BANDS):
        pl.semaphore_signal(
            barrier, inc=1, device_id=(af(xs[i // 8], from_y[i // 2 % 4], pair[i % 2]), row), device_id_type=MESH
        )

    sel_copy.wait()
    chosen = [sel_ref[o] - a * SHOTS for o in range(OUT)]
    flag = [sum((c == s).astype(I32) for c in chosen) for s in range(SHOTS)]
    count = sum(flag)
    place, ahead = [], 0
    for s in range(SHOTS):
        place.append(jnp.where(flag[s] > 0, ahead, count + s - ahead))
        ahead = ahead + flag[s]
    shot_at = [sum(jnp.where(place[s] == n, s, 0) for s in range(SHOTS)) for n in range(SHOTS)]

    fwd_copy.wait()
    live_copy.wait()
    for c in loads:
        c.wait()

    def band_of(bx, hy, hz):
        return bx * 8 + lax.rem(hy, 4) * 2 + lax.rem(hz, 2)

    to_slot = [x * 8 + lax.rem(y - base_of(hy) + NY, NY) * 2 + zs for hy in to_y]

    def band_copy(ph, dx, w, dz):
        band, slot = band_of(xs[dx], to_y[w], pair[dz]), to_slot[w]
        return pltpu.make_async_remote_copy(
            src_ref=sends[ph].at[band], dst_ref=recvs[ph].at[slot],
            send_sem=send_sem.at[(dx * 4 + w) * 2 + dz if ph < phases - 1 else 0],
            recv_sem=recv_sem.at[ph, slot], device_id=(af(xs[dx], to_y[w], pair[dz]), row), device_id_type=MESH,
        )

    own_band, own_slot = band_of(x, y, z), to_slot[0]
    own_copies = [
        pltpu.make_async_copy(sends[ph].at[own_band], recvs[ph].at[own_slot], own_sem.at[ph]) for ph in range(phases)
    ]
    order = [
        [((1 + 2 * i + j % 2) % NX, (j // 2 + 1) % 4, (j // 8 + 1) % 2) for j in range(16)] for i in range(2)
    ]
    order = [[t for t in part if t != (0, 0, 0)] for part in order]

    for ph in range(phases):
        for i in range(2):
            first = xs[(1 + 2 * i) % NX]
            second = xs[(2 + 2 * i) % NX]
            table = fwd[pl.ds(pl.multiple_of(first * 128, 128), 256), :]
            for n in range(*parts[ph]):
                shot = shot_at[n]
                spec = mm(table, traces[shot], ((1,), (1,))) * live_ref[pl.ds(shot, 1), :].astype(F32)
                spec = spec.astype(BF).reshape(2, 8, COMP, RECV)
                sends[ph][pl.ds(first * 8, 8), n - parts[ph][0]] = spec[0]
                sends[ph][pl.ds(second * 8, 8), n - parts[ph][0]] = spec[1]
            if ph == 0:
                if i == 0:
                    pl.semaphore_wait(barrier, BANDS - 1 + 1 + 3 + 1)
                    pl.semaphore_signal(homes_sem, inc=1, device_id=(a, other), device_id_type=MESH)
                for t in order[i]:
                    band_copy(0, *t).start()
        own_copies[ph].start()

    ro, co = iota((256, 256), 0), iota((256, 256), 1)
    n, s = ro % 16 // SHOTS, ro % SHOTS
    from_a, from_b = n * early + s, 2 * early + n * (SHOTS - early) + s - early
    turn[...] = jnp.where(co == jnp.where(s < early, from_a, from_b) * 16 + ro // 16, 1.0, 0.0).astype(BF)
    line = jnp.full((1, 128), -1, I32)
    for o in range(OUT):
        line = jnp.where(iota((1, 128), 1) == o, sel_ref[o], line)

    @pl.loop(0, OUT)
    def _(o):
        shot = sel_ref[o]
        owner = lax.div(shot, SHOTS)
        rank = sum(
            ((lax.div(sel_ref[p], SHOTS) == owner) & (sel_ref[p] < shot)).astype(I32) for p in range(OUT)
        )
        dy = lax.rem(lax.rem(lax.div(owner, NZ), NY) - base + NY, NY)
        oz = lax.rem(owner, NZ)
        src_ref[o] = lax.div(owner, NY * NZ) * 8 + lax.rem(dy, 4) * 2 + lax.rem(oz, 2)
        place_ref[o] = jnp.minimum(rank, early - 1)
        group_ref[o] = lax.div(dy, 4) * 2 + jnp.where(lax.div(oz, 2) == zp, 0, 1)

    per_cap = PER * cap
    to_pack = jnp.full((1, 512), -1, I32)
    to_expand = jnp.full((OUT, 128), 0, I32)
    counts = [0] * 4
    for o in range(OUT):
        group = group_ref[o]
        rank = sum(jnp.where(group == v, counts[v], 0) for v in range(4))
        counts = [counts[v] + (group == v).astype(I32) for v in range(4)]
        to_pack = jnp.where((iota((1, 512), 1) // COMP == o) & (group == 0), rank, to_pack)
        to_expand = jnp.where(iota((OUT, 128), 0) == o, group * per_cap + rank, to_expand)
    pr = iota((COMP * cap, 512), 0)
    pack[...] = jnp.where(
        (iota((COMP * cap, 512), 1) % COMP == pr // cap) & (to_pack == pr % cap), 1.0, 0.0
    ).astype(BF)
    for f in range(PER):
        expand[f * OUT : (f + 1) * OUT, :] = jnp.where(
            iota((OUT, 4 * per_cap), 1) == to_expand[:, 0:1] + f * cap, 1.0, 0.0
        ).astype(BF)

    r_at = iota((256, 128), 0)
    here = jnp.where((row * RECV + r_at == line) & (iota((256, 128), 1) < OUT), 1.0, 0.0)
    same = ro // SHOTS == co // SHOTS
    ahead_of = mm(jnp.where(same & (co < ro), 1.0, 0.0).astype(BF), here.astype(BF))
    all_of = mm(jnp.where(same, 1.0, 0.0).astype(BF), here.astype(BF))
    total_of = lambda v: jnp.sum(v, axis=1, keepdims=True).astype(I32)
    n_here, n_ahead, n_all = total_of(here), total_of(ahead_of), total_of(all_of)
    r1 = iota((256, 1), 0)
    at = jnp.where(n_here > 0, n_ahead, n_all + r1 % SHOTS - n_ahead)
    ry, rz = (r1 // (NZ * SHOTS) - base + NY) % NY, r1 // SHOTS % NZ
    u = ry // 4 * 2 + jnp.where(rz // 2 == zp, 0, 1)
    to = u * 128 + (ry % 4 * 2 + rz % 2) * SHOTS + at
    for p in range(2):
        lanes[p * 256 : (p + 1) * 256, :] = jnp.where(iota((256, 512), 1) == to + p * 64, 1.0, 0.0).astype(BF)
    d_at = iota((128, 512), 0)
    j2 = iota((128, 512), 1)
    spread[...] = jnp.where(j2 % 256 == 2 * d_at + j2 // 256, 1.0, 0.0).astype(BF)
    p2[...] = jnp.zeros_like(p2)

    def second_phase(start, stop):
        for t in (order[0] + order[1])[start:stop] if phases == 2 else ():
            band_copy(0, *t).wait_send()
            band_copy(1, *t).start()

    second_phase(0, METER[0])

    def await_from(ph, sx):
        for q in range(8):
            slot = sx * 8 + q

            @pl.when(slot != own_slot)
            def _():
                pltpu.make_async_remote_copy(
                    src_ref=sends[ph].at[0], dst_ref=recvs[ph].at[slot], send_sem=send_sem.at[0],
                    recv_sem=recv_sem.at[ph, slot], device_id=cores, device_id_type=MESH,
                ).wait_recv()

    def arrive(start, stop):
        @pl.loop(start, stop)
        def _(i):
            sx = lax.rem(x + 2 * NX - 1 - i, NX)
            if phases == 2:
                await_from(1, sx)
            for q in range(4):
                block = [
                    recvs[ph][pl.ds(sx * 8 + q * 2, 2)].reshape(-1, RECV) for ph in range(phases)
                ]
                turned = mm(turn[...], jnp.concatenate(block, axis=0)).astype(BF).reshape(2, PER, 16, RECV)
                bt[:, sx, 0, q] = turned[0]
                bt[:, sx, 1, q] = turned[1]

    for c in own_copies:
        c.wait()

    @pl.loop(0, NX)
    def _(i):
        await_from(0, lax.rem(x + 2 * NX - 1 - i, NX))

    def home_copy(side, v):
        sem = side * 4 + v
        return pltpu.make_async_remote_copy(
            src_ref=a_msg.at[v], dst_ref=a_in.at[side, v], send_sem=a_send_sem.at[sem],
            recv_sem=a_recv_sem.at[sem], device_id=(homes[v], (row, other)[side]), device_id_type=MESH,
        )

    def core_copy(slot, sem):
        return pltpu.make_async_remote_copy(
            src_ref=a_row.at[slot], dst_ref=a_row.at[slot], send_sem=row_send_sem.at[sem],
            recv_sem=row_recv_sem.at[sem], device_id=cores, device_id_type=MESH,
        )

    for o in range(OUT):
        picked[o] = recv_a[src_ref[o], place_ref[o]]
    got = mm(pack[...], picked[...].reshape(OUT * COMP, RECV)).astype(BF).reshape(2, PER, cap, RECV)
    for f in range(PER):
        a_own[f * cap : (f + 1) * cap, 0:RECV] = got[0, f]
        a_own[f * cap : (f + 1) * cap, RECV:] = got[1, f]
    pl.semaphore_wait(homes_sem, 1)
    for v in (3, 2, 1, 0):
        msg = mm(a_own[...], lanes[:, v * 128 : (v + 1) * 128]).astype(BF)
        a_msg[v] = msg
        home_copy(1, v).start()
        if v:
            home_copy(0, v).start()
        else:
            a_in[0, 0] = msg

    second_phase(METER[0], METER[1])

    if phases == 2 and METER[2]:
        arrive(0, METER[2])
    for v in (1, 2, 3):
        home_copy(0, v).wait()
    a_row[row] = mm(expand[...], a_in[0].reshape(4 * per_cap, 128)).astype(BF)
    near = core_copy(row, 0)
    near.start()
    for v in range(4):
        home_copy(1, v).wait()
    a_row[other] = mm(expand[...], a_in[1].reshape(4 * per_cap, 128)).astype(BF)
    far = core_copy(other, 1)
    far.start()
    second_phase(METER[1], BANDS)
    arrive(METER[2] if phases == 2 else 0, NX)
    near.wait_recv()
    far.wait_recv()

    imag = iota((1, 128), 1) >= 64
    sign = jnp.where(imag, -1.0, 1.0)
    factor = 1.0 / math.sqrt(NX * NY * NZ * SHOTS)
    left = []
    for v in range(NROW):
        val = a_row[v].astype(F32)
        left.append(((val * sign).astype(BF), pltpu.roll(val, 64, 1).astype(BF)))
    for f in range(PER):
        rows = slice(f * OUT, (f + 1) * OUT)
        lhs = jnp.concatenate(
            [jnp.concatenate([left[v][p][rows] for v in range(NROW)], axis=1) for p in range(2)], axis=0
        )
        pred = (mm(lhs, bt[f].reshape(512, RECV)) * factor).astype(BF)
        p2[f, 0:64, 0:RECV] = pred
        p2[f, 64:128, RECV:] = pred

    for f in range(PER):
        stage[pl.ds(f, 128, stride=8), :] = mm(spread[...], p2[f], ((1,), (1,)))
    r_send[...] = stage[...].astype(BF).reshape(128, 8, 128)

    my_slot = (lax.div(y, 4) * 2 + zp) * BANDS + own_band
    own_r = pltpu.make_async_copy(r_send.at[a], r_recv.at[my_slot], r_own_sem)
    own_r.start()

    def back(d):
        pltpu.make_async_remote_copy(
            src_ref=r_send.at[d], dst_ref=r_recv.at[my_slot], send_sem=r_send_sem,
            recv_sem=r_recv_sem, device_id=(d, row), device_id_type=MESH,
        ).start()

    @pl.loop(0, NX)
    def _(i):
        dx = lax.rem(x + 2 + i, NX)
        for j in range(31):
            back(af(dx, ys[(4, 3, 5, 2, 6, 1, 7, 0)[j % NY]], zz[(2, 1, 3, 0)[j // NY]]))

        @pl.when(i != 2)
        def _():
            back(af(dx, y, z))

    all_r = pltpu.make_async_remote_copy(
        src_ref=r_send.at[pl.ds(0, 127)], dst_ref=r_recv.at[pl.ds(0, 127)], send_sem=r_send_sem,
        recv_sem=r_recv_sem, device_id=cores, device_id_type=MESH,
    )
    inv_copy.wait()
    own_r.wait()
    all_r.wait_recv()

    total = r_recv[0:32].astype(F32)
    for v in range(1, 4):
        total = total + r_recv[v * 32 : (v + 1) * 32].astype(F32)
    turned = total.reshape(256, 128).T.astype(BF)
    lhs = jnp.concatenate(
        [jnp.concatenate([turned[r * 64 : r * 64 + 32], turned[r * 64 + 32 : r * 64 + 64]], axis=1) for r in range(2)],
        axis=0,
    )
    res = mm(lhs, inv[...])
    for r in range(2):
        out_ref[r] = res[r * 32 : (r + 1) * 32]

    all_r.wait_send()
    near.wait_send()
    far.wait_send()
    pltpu.make_async_remote_copy(
        src_ref=sends[phases - 1].at[pl.ds(0, 31)], dst_ref=recvs[phases - 1].at[pl.ds(0, 31)],
        send_sem=send_sem.at[0], recv_sem=recv_sem.at[0, 0], device_id=cores, device_id_type=MESH,
    ).wait_send()


def per_device(traces, live, selected):
    fwd, inv = host_tables()
    any_, vmem = pl.BlockSpec(memory_space=pl.ANY), pl.BlockSpec(memory_space=pltpu.VMEM)
    dma = pltpu.SemaphoreType.DMA

    def call(early, cap):
        late = max(SHOTS - early, 1)
        return pl.pallas_call(
            functools.partial(kernel, early, cap),
            out_shape=jax.ShapeDtypeStruct((2, OUT, NT), F32),
            in_specs=[any_] * 5,
            out_specs=vmem,
            scratch_shapes=[
                pltpu.SMEM((OUT,), I32),
                pltpu.SMEM((OUT,), I32),
                pltpu.SMEM((OUT,), I32),
                pltpu.SMEM((OUT,), I32),
                pltpu.VMEM((SHOTS, RECV), I32),
                pltpu.VMEM((SHOTS, RECV, NT), BF),
                pltpu.VMEM((2 * NF + 128, NT), BF),
                pltpu.VMEM((2 * NF, NT), BF),
                pltpu.VMEM((BANDS, early, COMP, RECV), BF),
                pltpu.VMEM((BANDS, late, COMP, RECV), BF),
                pltpu.VMEM((BANDS, early, COMP, RECV), BF),
                pltpu.VMEM((BANDS, late, COMP, RECV), BF),
                pltpu.VMEM((PER, NX, 2, 4, 16, RECV), BF),
                pltpu.VMEM((256, 256), BF),
                pltpu.VMEM((COMP * cap, 512), BF),
                pltpu.VMEM((OUT, COMP, RECV), BF),
                pltpu.VMEM((512, 512), BF),
                pltpu.VMEM((PER * OUT, 4 * PER * cap), BF),
                pltpu.VMEM((128, 512), BF),
                pltpu.VMEM((PER * cap, 512), BF),
                pltpu.VMEM((4, PER * cap, 128), BF),
                pltpu.VMEM((2, 4, PER * cap, 128), BF),
                pltpu.VMEM((NROW, PER * OUT, 128), BF),
                pltpu.VMEM((PER, 128, 512), BF),
                pltpu.VMEM((1024, 128), F32),
                pltpu.VMEM((128, 8, 128), BF),
                pltpu.VMEM((128, 8, 128), BF),
                dma((SHOTS + 4,)), dma((BANDS,)), dma((2, BANDS)), dma((2,)),
                dma((8,)), dma((8,)), dma((2,)), dma((2,)),
                dma, dma, dma, pltpu.SemaphoreType.REGULAR,
            ],
            compiler_params=pltpu.CompilerParams(
                collective_id=early, has_side_effects=True, vmem_limit_bytes=60 << 20
            ),
            cost_estimate=pl.CostEstimate(flops=2 << 30, bytes_accessed=4 << 20, transcendentals=0),
            name="multiples",
        )(selected, traces, live, jnp.asarray(fwd), jnp.asarray(inv))

    owner = selected // SHOTS
    zone = owner // NZ % NY // 2 * 2 + owner % NZ // 2
    at = jnp.arange(8, dtype=I32)[:, None]
    member = (zone[None, :] == at) | (zone[None, :] == (at + 2) % 8)
    held = jnp.concatenate([(owner[:, None] == owner[None, :]).astype(I32) * (CAP + 1), member.astype(I32) * (EARLY + 1)])
    fits = jnp.max(jnp.sum(held, axis=1)) < (CAP + 1) * (EARLY + 1)
    out = lax.cond(fits, lambda: call(EARLY, CAP), lambda: call(SHOTS, OUT))
    return out.transpose(1, 0, 2)[:, None]


def solution(mesh):
    in_specs = (P("af", "row", None), P("af", "row"), P())
    out_specs = P(None, "row", "af", None)
    return jax.shard_map(per_device, mesh=mesh, in_specs=in_specs, out_specs=out_specs, check_vma=False)
```

time: 68.5 us -> 67.1 us (0.980)
  Pallas kernels: 65.4 us -> 63.8 us
    pallas_call x1, Pallas kernels: 65.4 us -> 63.8 us  [call(): pl.pallas_call(functools.partial(kernel, early, cap), out_shape=jax.Shape...]
    add x0 -> x1, other arithmetic: none -> 0.69 us  [per_device(): zone = owner // NZ % NY // 2 * 2 + owner % NZ // 2]
where the time goes in v5:
time: 67.1 us; the launch traced here: 67 us
  Pallas kernels  63.8 us (95%)
  other arithmetic  1.57 us (2%)
  local copies, waits for them, and re-layouts  0.76 us (1%)
    pallas_call x1, Pallas kernels, call(): pl.pallas_call(functools.partial(kernel, early, cap), out_shape=jax.Shape...  63.8 us

profile of v5, /device:TPU:1, one launch (start us, length us, event | category | flops | bytes accessed | tf_op | source)
XLA Modules:
  0.0 67.0 jit_solution(8702900217040480719)
XLA Ops:
  0.0 0.7 %fusion.4 = (s32[32]{0:T(128)S(1)}, s32[32]{0:T(128)S(1)}) fusion(s32[32]{0:T(128)} %param.9), kind=kLoop, calls=%fused_computation.31 | loop fusion | flops 2464 | bytes 384 | tf_op jit(solution)/shard_map/add | solution.py:425
  0.7 0.1 fusion.1
  0.8 0.1 compare_select_fusion
  0.8 0.1 add_reduce_fusion
  0.9 0.6 reduce_max.9
  2.2 64.0 %conditional.1 = (f32[2,32,512]{2,1,0:T(8,128)S(1)}) conditional(s32[]{:T(128)} %convert_element_type.2, (s32[32]{0:T(128)}, bf16[8,256,512]{2,1,0:T(8,128)(2,1)}, s32[8,256]{1,0:T(8,128)}, bf16[640,512]{1,0:T(8,128)(2,1)}, bf16[512,512]{1,0:T(8,128)(2,1)}) %tuple.11, (s32[32]{0:T(128)}, bf16[8,256,512]{2,1,0:T(8,128)(2,1)}, s32[8,256]{1,0:T(8,128)}, ...), branch_computations={%region_2.3_spmd, %region_3.4_spmd} | conditional | flops 2147483648 | bytes 4194312 | solution.py:430
  2.4 63.8 %multiples.3 = f32[2,32,512]{2,1,0:T(8,128)S(1)} custom-call(s32[32]{0:T(128)} %get-tuple-element.33.sel_hbm, bf16[8,256,512]{2,1,0:T(8,128)(2,1)} %get-tuple-element.34.traces_hbm, s32[8,256]{1,0:T(8,128)} %get-tuple-element.35.live_hbm, bf16[640,512]{1,0:T(8,128)(2,1)} %get-tuple-element.36.fwd_hbm, bf16[512,512]{1,0:T(8,128)(2,1)} %get-tuple-element.37.inv_hbm), custom_call_target="tpu_custom_call" | custom-call | flops 2147483648 | bytes 4194304 | tf_op jit(solution)/shard_map/cond/branch_1_fun/multiples/pallas_call | solution.py:380
  66.2 0.8 %copy.9 = f32[2,32,512]{2,0,1:T(2,128)} copy(f32[2,32,512]{2,1,0:T(8,128)S(1)} %get-tuple-element.40) | data formatting | bytes 262144 | tf_op jit(solution)/shard_map/cond | solution.py:430
  (1 shorter events, 0.0 us)

commit v6 on v5

--- a/solution.py
+++ b/solution.py
@@ -134,7 +134,8 @@
     order = [
         [((1 + 2 * i + j % 2) % NX, (j // 2 + 1) % 4, (j // 8 + 1) % 2) for j in range(16)] for i in range(2)
     ]
-    order = [[t for t in part if t != (0, 0, 0)] for part in order]
+    hops = lambda t: min(t[0], NX - t[0]) + (0, 1, 2, 1)[t[1]] + t[2]
+    order = [sorted([t for t in part if t != (0, 0, 0)], key=hops, reverse=True) for part in order]
 
     for ph in range(phases):
         for i in range(2):
@@ -359,7 +360,7 @@
     )
     res = mm(lhs, inv[...])
     for r in range(2):
-        out_ref[r] = res[r * 32 : (r + 1) * 32]
+        out_ref[:, 0, r, :] = res[r * 32 : (r + 1) * 32]
 
     all_r.wait_send()
     near.wait_send()
@@ -379,7 +380,7 @@
         late = max(SHOTS - early, 1)
         return pl.pallas_call(
             functools.partial(kernel, early, cap),
-            out_shape=jax.ShapeDtypeStruct((2, OUT, NT), F32),
+            out_shape=jax.ShapeDtypeStruct((OUT, 1, 2, NT), F32),
             in_specs=[any_] * 5,
             out_specs=vmem,
             scratch_shapes=[
@@ -428,7 +429,7 @@
     held = jnp.concatenate([(owner[:, None] == owner[None, :]).astype(I32) * (CAP + 1), member.astype(I32) * (EARLY + 1)])
     fits = jnp.max(jnp.sum(held, axis=1)) < (CAP + 1) * (EARLY + 1)
     out = lax.cond(fits, lambda: call(EARLY, CAP), lambda: call(SHOTS, OUT))
-    return out.transpose(1, 0, 2)[:, None]
+    return out
 
 
 def solution(mesh):

time: 67.1 us -> 66.7 us (level)
    cond x1 -> x0, local copies, waits for them, and re-layouts: 0.76 us -> none  [per_device(): out = lax.cond(fits, lambda: call(EARLY, CAP), lambda: call(SHOTS, OUT))]
where the time goes in v6:
time: 66.7 us; the launch traced here: 66.5 us
  Pallas kernels  63.4 us (95%)
  other arithmetic  1.57 us (2%)
  between operations  0.67 us (1%)
    pallas_call x1, Pallas kernels, call(): pl.pallas_call(functools.partial(kernel, early, cap), out_shape=jax.Shape...  63.4 us

profile of v6, /device:TPU:1, one launch (start us, length us, event | category | flops | bytes accessed | tf_op | source)
XLA Modules:
  0.0 66.5 jit_solution(15933209897217091525)
XLA Ops:
  0.0 0.7 %fusion.4 = (s32[32]{0:T(128)S(1)}, s32[32]{0:T(128)S(1)}) fusion(s32[32]{0:T(128)} %param.9), kind=kLoop, calls=%fused_computation.30 | loop fusion | flops 2464 | bytes 384 | tf_op jit(solution)/shard_map/add | solution.py:426
  0.7 0.1 fusion.1
  0.8 0.1 compare_select_fusion
  0.8 0.1 add_reduce_fusion
  0.9 0.6 reduce_max.9
  2.2 63.6 %conditional.1 = (f32[32,1,2,512]{3,2,1,0:T(2,128)S(1)}) conditional(s32[]{:T(128)} %convert_element_type.2, (s32[32]{0:T(128)}, bf16[8,256,512]{2,1,0:T(8,128)(2,1)}, s32[8,256]{1,0:T(8,128)}, bf16[640,512]{1,0:T(8,128)(2,1)}, bf16[512,512]{1,0:T(8,128)(2,1)}) %tuple.11, (s32[32]{0:T(128)}, bf16[8,256,512]{2,1,0:T(8,128)(2,1)}, s32[8,256]{1,0:T(8,128)}, ...), branch_computations={%region_2.3_spmd, %region_3.4_spmd} | conditional | flops 2147483648 | bytes 4194312 | solution.py:431
  2.4 63.4 %multiples.3 = f32[32,1,2,512]{3,2,1,0:T(2,128)S(1)} custom-call(s32[32]{0:T(128)} %get-tuple-element.33.sel_hbm, bf16[8,256,512]{2,1,0:T(8,128)(2,1)} %get-tuple-element.34.traces_hbm, s32[8,256]{1,0:T(8,128)} %get-tuple-element.35.live_hbm, bf16[640,512]{1,0:T(8,128)(2,1)} %get-tuple-element.36.fwd_hbm, bf16[512,512]{1,0:T(8,128)(2,1)} %get-tuple-element.37.inv_hbm), custom_call_target="tpu_custom_call" | custom-call | flops 2147483648 | bytes 4194304 | tf_op jit(solution)/shard_map/cond/branch_1_fun/multiples/pallas_call | solution.py:381
  65.9 0.7 copy.11
  (1 shorter events, 0.0 us)
